TPU v7x, 128 devices: a whole 4x4x4 slice. The times are simulated.
128 devices in a mesh: pt: 16 (over y, x), ct: 8 (over z, core).
Axes of the slice: x: 4, y: 4, z: 4, core: 2. Of those that a mesh axis runs over, the one named last changes fastest.
Arguments:
- points: float32 [32768, 128], P('pt'), may hold values from -8 to 8, as said below
- centroids: float32 [16384, 128], P('ct'), may hold values from -4 to 4, as said below
- cotangent: float32 [32768, 128], P('pt'), may hold values from -6 to 6
Outputs:
- point_grad: float32 [32768, 128], P(('pt', 'ct'))
- centroid_grad_out: float32 [16384, 128], P('ct')
Inputs may be any that keep to these rules, and one draw needn't show every extreme that they name: `points`: embedding entries of order one. `centroids`: centroid entries of order one.
All inputs are finite; a program needn't handle non-finite values.
Results may differ from a plain program's by a relative error of at most 0.0003.
Values sent between devices are 32-bit elements; how exact they have to be, the bound alone decides.
No kernel may reach another device: no remote copies, remote signals or barrier semaphores. Data moves between devices by JAX's collectives and lax.ppermute only.
A program may use at most 128 MiB of HBM per device.

v0:
```python
import math

import jax
import jax.numpy as jnp
from jax import lax
from jax.sharding import PartitionSpec as P

BLOCK = 512


def combine_pair(first, second):
    peak = jnp.maximum(first[0], second[0])
    total = first[1] * jnp.exp(first[0] - peak) + second[1] * jnp.exp(second[0] - peak)
    return (peak, total)


def row_global(peak, total):
    top = lax.pmax(peak, "ct")
    total = lax.psum(total * jnp.exp(peak - top), "ct")
    peak = top
    return peak + jnp.log(total)


def col_global(peak, total):
    top = lax.pmax(peak, "pt")
    total = lax.psum(total * jnp.exp(peak - top), "pt")
    peak = top
    return peak + jnp.log(total)


def per_device(points, centroids, cotangent):
    rows, width = points.shape
    cols = centroids.shape[0]
    ratio_log = math.log(rows * lax.axis_size("pt") / (cols * lax.axis_size("ct")))
    ratio = cols * lax.axis_size("ct") / (rows * lax.axis_size("pt"))
    scale = 3.0 / math.sqrt(width)
    block = min(BLOCK, rows)
    count = rows // block
    highest = lax.Precision.HIGHEST

    def compute_scores(index):
        block_rows = points[index * block : (index + 1) * block]
        return scale * jnp.dot(
            block_rows, centroids.T, precision=highest, preferred_element_type=jnp.float32
        )

    def scores(index):
        return compute_scores(index)

    def row_pass(col_shift):
        peaks = []
        totals = []
        for index in range(count):
            shifted = scores(index) + col_shift[None, :]
            peak = jnp.max(shifted, axis=1)
            peaks.append(peak)
            totals.append(jnp.sum(jnp.exp(shifted - peak[:, None]), axis=1))
        return row_global(jnp.concatenate(peaks), jnp.concatenate(totals))

    def col_pass(row_shift):
        stats = None
        for index in range(count):
            shifted = scores(index) + row_shift[index * block : (index + 1) * block, None]
            peak = jnp.max(shifted, axis=0)
            fresh = (peak, jnp.sum(jnp.exp(shifted - peak[None, :]), axis=0))
            stats = fresh if stats is None else combine_pair(stats, fresh)
        return col_global(stats[0], stats[1])

    zero_cols = jnp.zeros((cols,), jnp.float32)
    f1 = -row_pass(zero_cols)
    g1 = ratio_log - col_pass(f1)
    f2 = -row_pass(g1)
    g2 = ratio_log - col_pass(f2)

    def piece(vector, index):
        return vector[index * block : (index + 1) * block]

    col_edge = jnp.zeros((cols,), jnp.float32)
    direct = jnp.zeros((cols, width), jnp.float32)
    row_parts = []
    for index in range(count):
        plan = jnp.exp(scores(index) + piece(f2, index)[:, None] + g2[None, :])
        cot = cotangent[index * block : (index + 1) * block]
        wmat = jnp.dot(cot, centroids.T, precision=highest, preferred_element_type=jnp.float32)
        edge = plan * wmat
        row_parts.append(jnp.sum(edge, axis=1))
        col_edge = col_edge + jnp.sum(edge, axis=0)
        direct = direct + jnp.einsum("ij,id->jd", plan, cot, precision=highest)
    row_edge, dg2 = (lax.psum(jnp.concatenate(row_parts), "ct"), lax.psum(col_edge, "pt"))
    weighted_parts = []
    for index in range(count):
        plan = jnp.exp(scores(index) + piece(f2, index)[:, None] + g2[None, :])
        weighted_parts.append(jnp.sum(plan * dg2[None, :], axis=1))
    df2 = row_edge - ratio * lax.psum(jnp.concatenate(weighted_parts), "ct")
    col_back = jnp.zeros((cols,), jnp.float32)
    for index in range(count):
        second = jnp.exp(scores(index) + g1[None, :] + piece(f2, index)[:, None])
        col_back = col_back - jnp.sum(second * piece(df2, index)[:, None], axis=0)
    dg1 = lax.psum(col_back, "pt")
    back_parts = []
    for index in range(count):
        first = jnp.exp(scores(index) + piece(f1, index)[:, None] + g1[None, :] - ratio_log)
        back_parts.append(-jnp.sum(first * dg1[None, :], axis=1))
    df1 = lax.psum(jnp.concatenate(back_parts), "ct")
    rest = jnp.zeros((cols, width), jnp.float32)
    point_terms = []
    for index in range(count):
        zval = scores(index)
        s1 = piece(f1, index)[:, None]
        s2 = piece(f2, index)[:, None]
        plan = jnp.exp(zval + s2 + g2[None, :])
        cot = cotangent[index * block : (index + 1) * block]
        wmat = jnp.dot(cot, centroids.T, precision=highest, preferred_element_type=jnp.float32)
        dz = plan * wmat - ratio * plan * dg2[None, :]
        dz = dz - jnp.exp(zval + g1[None, :] + s2) * piece(df2, index)[:, None]
        dz = dz - jnp.exp(zval + s1 + g1[None, :] - ratio_log) * dg1[None, :]
        dz = dz - jnp.exp(zval + s1) * piece(df1, index)[:, None]
        point_terms.append(
            scale * jnp.dot(dz, centroids, precision=highest, preferred_element_type=jnp.float32)
        )
        block_rows = points[index * block : (index + 1) * block]
        rest = rest + scale * jnp.einsum("ij,id->jd", dz, block_rows, precision=highest)
    point_term = jnp.concatenate(point_terms, axis=0)
    point_grad = lax.psum_scatter(point_term, "ct", scatter_dimension=0, tiled=True)
    centroid_grad_out = lax.psum(direct + rest, "pt")
    return (point_grad, centroid_grad_out)


def solution(mesh):
    return jax.shard_map(
        per_device,
        mesh=mesh,
        in_specs=(P("pt", None), P("ct", None), P("pt", None)),
        out_specs=(P(("pt", "ct"), None), P("ct", None)),
        check_vma=False,
    )
```

profile of v0, /device:TPU:0, one launch (start us, length us, event | category | flops | bytes accessed | tf_op | source)
XLA Modules:
  0.0 608.2 jit_solution(5205309928992734465)
XLA Ops:
  9.2 6.1 fusion.42
  30.7 16.2 %pmax.28 = f32[2048]{0:T(1024)S(1)} all-reduce(f32[2048]{0:T(1024)S(1)} %pad_maximum_fusion.1), channel_id=1, replica_groups=mesh['pt'=16,'ct'=8] {'ct'}, use_global_device_ids=true, to_apply=%region_4.0 | all-reduce | flops 2048 | bytes 16384 | tf_op jit(solution)/shard_map/pmax | solution.py:18
  54.2 13.1 %psum.70 = f32[2048]{0:T(1024)S(1)} all-reduce(f32[2048]{0:T(1024)S(1)} %maximum_multiply_fusion), channel_id=1, replica_groups=mesh['pt'=16,'ct'=8] {'ct'}, use_global_device_ids=true, to_apply=%region_9.0 | all-reduce | flops 2048 | bytes 16384 | tf_op jit(solution)/shard_map/psum | solution.py:19
  77.6 41.2 %pmax.29 = f32[2048]{0:T(1024)S(1)} all-reduce(f32[2048]{0:T(1024)S(1)} %get-tuple-element.34), channel_id=1, replica_groups=mesh['pt'=16,'ct'=8] {'pt'}, use_global_device_ids=true, to_apply=%region_14.0 | all-reduce | flops 2048 | bytes 16384 | tf_op jit(solution)/shard_map/pmax | solution.py:25
  118.8 36.0 %psum.71 = f32[2048]{0:T(1024)S(1)} all-reduce(f32[2048]{0:T(1024)S(1)} %exponential_multiply_fusion.9), channel_id=1, replica_groups=mesh['pt'=16,'ct'=8] {'pt'}, use_global_device_ids=true, to_apply=%region_19.0 | all-reduce | flops 2048 | bytes 16384 | tf_op jit(solution)/shard_map/psum | solution.py:26
  158.2 5.7 exponential_reduce_fusion.7
  167.9 12.7 %pmax.30 = f32[2048]{0:T(1024)S(1)} all-reduce(f32[2048]{0:T(1024)S(1)} %pad_maximum_fusion.2), channel_id=1, replica_groups=mesh['pt'=16,'ct'=8] {'ct'}, use_global_device_ids=true, to_apply=%region_24.0 | all-reduce | flops 2048 | bytes 16384 | tf_op jit(solution)/shard_map/pmax | solution.py:18
  180.6 12.7 %psum.72 = f32[2048]{0:T(1024)S(1)} all-reduce(f32[2048]{0:T(1024)S(1)} %maximum_multiply_fusion.1), channel_id=1, replica_groups=mesh['pt'=16,'ct'=8] {'ct'}, use_global_device_ids=true, to_apply=%region_29.0 | all-reduce | flops 2048 | bytes 16384 | tf_op jit(solution)/shard_map/psum | solution.py:19
  203.5 38.1 %pmax.31 = f32[2048]{0:T(1024)S(1)} all-reduce(f32[2048]{0:T(1024)S(1)} %get-tuple-element.31), channel_id=1, replica_groups=mesh['pt'=16,'ct'=8] {'pt'}, use_global_device_ids=true, to_apply=%region_34.0 | all-reduce | flops 2048 | bytes 16384 | tf_op jit(solution)/shard_map/pmax | solution.py:25
  241.7 36.0 %psum.73 = f32[2048]{0:T(1024)S(1)} all-reduce(f32[2048]{0:T(1024)S(1)} %exponential_multiply_fusion.8), channel_id=1, replica_groups=mesh['pt'=16,'ct'=8] {'pt'}, use_global_device_ids=true, to_apply=%region_39.0 | all-reduce | flops 2048 | bytes 16384 | tf_op jit(solution)/shard_map/psum | solution.py:26
  277.7 7.5 %fusion.32 = (f32[2048]{0:T(1024)S(1)}, f32[512]{0:T(512)S(1)}, f32[512,2048]{1,0:T(8,128)}) fusion(f32[2048,128]{1,0:T(8,128)S(1)} %copy-done, f32[2048,128]{1,0:T(8,128)S(1)} %copy-done.29, f32[2048]{0:T(1024)S(1)} %add_subtract_fusion, f32[512,2048]{1,0:T(8,128)} %get-tuple-element.62, f32[512]{0:T(512)S(1)} %get-tuple-element.49), kind=kOutput, calls=%fused_computation.116 | convolution fusion | flops 1615853056 | bytes 9719808 | tf_op jit(solution)/shard_map/dot_general | solution.py:84
  285.2 5.8 fusion.34
  291.0 5.8 fusion.35
  296.8 5.8 fusion.33
  302.6 38.2 %psum.74 = f32[2048]{0:T(1024)S(1)} all-reduce(f32[2048]{0:T(1024)S(1)} %add_add_fusion), channel_id=1, replica_groups=mesh['pt'=16,'ct'=8] {'pt'}, use_global_device_ids=true, to_apply=%region_44.0 | all-reduce | flops 2048 | bytes 16384 | tf_op jit(solution)/shard_map/psum | solution.py:89
  340.8 7.8 %multiply_reduce_fusion.3 = (f32[512]{0:T(512)S(1)}, f32[512]{0:T(512)S(1)}, f32[512]{0:T(512)S(1)}, f32[512]{0:T(512)S(1)}) fusion(f32[2048]{0:T(1024)S(1)} %psum.74, f32[2048]{0:T(1024)S(1)} %add_subtract_fusion, f32[512,2048]{1,0:T(8,128)} %get-tuple-element.64, f32[512]{0:T(512)S(1)} %get-tuple-element.52, f32[512,2048]{1,0:T(8,128)} %get-tuple-element.62, ...), kind=kLoop, calls=%fused_computation.18 | loop fusion | flops 16775168 | bytes 16809984 | tf_op jit(solution)/shard_map/reduce_sum | solution.py:93
  348.6 6.9 %fusion.10 = f32[2048,128]{1,0:T(8,128)S(1)} fusion(f32[512,2048]{1,0:T(8,128)S(1)} %copy-done.20, f32[2048]{0:T(1024)S(1)} %add_subtract_fusion, f32[512]{0:T(512)S(1)} %get-tuple-element.52, f32[2048,128]{1,0:T(8,128)S(1)} %copy-done.29), kind=kOutput, calls=%fused_computation.72 | convolution fusion | flops 1612709888 | bytes 5515264 | tf_op jit(solution)/shard_map/ij,id->jd/dot_general | solution.py:88
  355.6 23.6 %all-reduce = (f32[2048]{0:T(1024)S(1)}, f32[2048]{0:T(1024)S(1)}) all-reduce(f32[2048]{0:T(1024)S(1)} %pad_maximum_fusion.3, f32[2048]{0:T(1024)S(1)} %pad_maximum_fusion.4), channel_id=1, replica_groups=mesh['pt'=16,'ct'=8] {'ct'}, use_global_device_ids=true, to_apply=%region_49.0 | all-reduce | flops 4096 | bytes 32768 | tf_op jit(solution)/shard_map/psum | solution.py:89
  379.2 7.8 %fusion.4 = (f32[2048]{0:T(1024)S(1)}, f32[2048]{0:T(1024)S(1)}, f32[2048]{0:T(1024)S(1)}, f32[2048]{0:T(1024)S(1)}) fusion(f32[512,2048]{1,0:T(8,128)} %get-tuple-element.64, f32[512]{0:T(512)S(1)} %get-tuple-element.48, f32[512]{0:T(512)S(1)} %get-tuple-element.52, f32[2048]{0:T(1024)S(1)} %add_subtract_fusion.1, f32[512]{0:T(512)S(1)} %get-tuple-element.46, ...), kind=kLoop, calls=%fused_computation.60 | loop fusion | flops 16769024 | bytes 16834560 | tf_op jit(solution)/shard_map/reduce_sum | solution.py:98
  387.0 36.0 %psum.77 = f32[2048]{0:T(1024)S(1)} all-reduce(f32[2048]{0:T(1024)S(1)} %subtract_subtract_fusion), channel_id=1, replica_groups=mesh['pt'=16,'ct'=8] {'pt'}, use_global_device_ids=true, to_apply=%region_59.0 | all-reduce | flops 2048 | bytes 16384 | tf_op jit(solution)/shard_map/psum | solution.py:99
  423.0 8.0 %fusion.3 = (f32[512]{0:T(512)S(1)}, f32[512]{0:T(512)S(1)}, f32[512]{0:T(512)S(1)}, f32[512]{0:T(512)S(1)}) fusion(f32[512,2048]{1,0:T(8,128)} %get-tuple-element.64, f32[2048]{0:T(1024)S(1)} %psum.77, f32[2048]{0:T(1024)S(1)} %add_subtract_fusion.1, f32[512]{0:T(512)S(1)} %get-tuple-element.56, f32[512,2048]{1,0:T(8,128)} %get-tuple-element.62, ...), kind=kLoop, calls=%fused_computation.14 | loop fusion | flops 20969472 | bytes 16809984 | tf_op jit(solution)/shard_map/reduce_sum | solution.py:103
  431.0 12.7 %psum.78 = f32[2048]{0:T(1024)S(1)} all-reduce(f32[2048]{0:T(1024)S(1)} %pad_maximum_fusion.5), channel_id=1, replica_groups=mesh['pt'=16,'ct'=8] {'ct'}, use_global_device_ids=true, to_apply=%region_64.0 | all-reduce | flops 2048 | bytes 16384 | tf_op jit(solution)/shard_map/psum | solution.py:104
  443.7 11.5 %multiply_subtract_fusion.3 = (f32[512,2048]{1,0:T(8,128)S(1)}, f32[512,2048]{1,0:T(8,128)S(1)}) fusion(f32[512,2048]{1,0:T(8,128)} %get-tuple-element.68, f32[512,2048]{1,0:T(8,128)} %get-tuple-element.64, f32[512]{0:T(512)S(1)} %get-tuple-element.41, f32[2048]{0:T(1024)S(1)} %psum.77, f32[512]{0:T(512)S(1)} %get-tuple-element.48, ...), kind=kLoop, calls=%fused_computation.3 | loop fusion | flops 31457280 | bytes 25214976 | tf_op jit(solution)/shard_map/sub | solution.py:117
  457.3 6.7 %fusion.29 = f32[2048,128]{1,0:T(8,128)S(1)} fusion(f32[512,2048]{1,0:T(8,128)S(1)} %get-tuple-element.37, f32[2048,128]{1,0:T(8,128)S(1)} %copy-done.31), kind=kOutput, calls=%fused_computation.96 | convolution fusion | flops 1610612736 | bytes 5505024 | tf_op jit(solution)/shard_map/ij,id->jd/dot_general | solution.py:122
  464.0 7.2 %convolution_add_fusion.5 = f32[2048,128]{1,0:T(8,128)S(1)} fusion(f32[2048,128]{1,0:T(8,128)S(1)} %fusion.10, f32[512,2048]{1,0:T(8,128)S(1)} %copy-done.10, f32[2048]{0:T(1024)S(1)} %add_subtract_fusion, f32[512]{0:T(512)S(1)} %get-tuple-element.49, f32[2048,128]{1,0:T(8,128)S(1)} %copy-done.29), kind=kOutput, calls=%fused_computation.71 | convolution fusion | flops 1612972032 | bytes 6563840 | tf_op jit(solution)/shard_map/ij,id->jd/dot_general | solution.py:88
  471.3 7.0 %convolution_add_fusion.4 = f32[2048,128]{1,0:T(8,128)S(1)} fusion(f32[2048,128]{1,0:T(8,128)S(1)} %convolution_add_fusion.5, f32[512,2048]{1,0:T(8,128)S(1)} %copy-done.5, f32[2048]{0:T(1024)S(1)} %add_subtract_fusion, f32[512]{0:T(512)S(1)} %get-tuple-element.51, f32[2048,128]{1,0:T(8,128)S(1)} %copy-done.29), kind=kOutput, calls=%fused_computation.70 | convolution fusion | flops 1612972032 | bytes 6563840 | tf_op jit(solution)/shard_map/ij,id->jd/dot_general | solution.py:88
  478.3 7.4 %convolution_add_fusion.3 = f32[2048,128]{1,0:T(8,128)S(1)} fusion(f32[2048,128]{1,0:T(8,128)S(1)} %convolution_add_fusion.4, f32[512,2048]{1,0:T(8,128)S(1)} %copy-done.15, f32[2048]{0:T(1024)S(1)} %add_subtract_fusion, f32[512]{0:T(512)S(1)} %get-tuple-element.50, f32[2048,128]{1,0:T(8,128)S(1)} %copy-done.29), kind=kOutput, calls=%fused_computation.69 | convolution fusion | flops 1612972032 | bytes 6563840 | tf_op jit(solution)/shard_map/ij,id->jd/dot_general | solution.py:88
  485.7 8.4 %multiply_subtract_fusion.2 = (f32[512,2048]{1,0:T(8,128)S(1)}, f32[512,2048]{1,0:T(8,128)S(1)}) fusion(f32[512,2048]{1,0:T(8,128)S(1)} %copy-done.27, f32[512,2048]{1,0:T(8,128)S(1)} %copy-done.10, f32[512]{0:T(512)S(1)} %get-tuple-element.44, f32[2048]{0:T(1024)S(1)} %psum.77, f32[512]{0:T(512)S(1)} %get-tuple-element.45, ...), kind=kLoop, calls=%fused_computation.2 | loop fusion | flops 31457280 | bytes 25214976 | tf_op jit(solution)/shard_map/sub | solution.py:117
  494.1 6.9 %convolution_add_fusion.2 = f32[2048,128]{1,0:T(8,128)S(1)} fusion(f32[2048,128]{1,0:T(8,128)S(1)} %fusion.29, f32[512,2048]{1,0:T(8,128)S(1)} %get-tuple-element.39, f32[2048,128]{1,0:T(8,128)S(1)} %copy-done.31), kind=kOutput, calls=%fused_computation.68 | convolution fusion | flops 1610874880 | bytes 6553600 | tf_op jit(solution)/shard_map/ij,id->jd/dot_general | solution.py:122
  501.0 7.1 %convolution_add_fusion.1 = f32[2048,128]{1,0:T(8,128)S(1)} fusion(f32[2048,128]{1,0:T(8,128)S(1)} %convolution_add_fusion.2, f32[512,2048]{1,0:T(8,128)S(1)} %get-tuple-element.40, f32[2048,128]{1,0:T(8,128)S(1)} %copy-done.31), kind=kOutput, calls=%fused_computation.67 | convolution fusion | flops 1610874880 | bytes 6553600 | tf_op jit(solution)/shard_map/ij,id->jd/dot_general | solution.py:122
  508.1 7.7 %fusion.9 = f32[2048,128]{1,0:T(8,128)} fusion(f32[2048,128]{1,0:T(8,128)S(1)} %convolution_add_fusion.3, f32[2048,128]{1,0:T(8,128)S(1)} %convolution_add_fusion.1, f32[512,2048]{1,0:T(8,128)S(1)} %get-tuple-element.38, f32[2048,128]{1,0:T(8,128)S(1)} %copy-done.31), kind=kOutput, calls=%fused_computation.66 | convolution fusion | flops 1611399168 | bytes 7602176 | tf_op jit(solution)/shard_map/ij,id->jd/dot_general | solution.py:122
  534.9 63.3 %all-reduce.3.cloned.1.call-done = f32[2048,128]{1,0:T(8,128)} async-done(((f32[2048,128]{1,0:T(8,128)}), f32[2048,128]{1,0:T(8,128)}) %all-reduce.3.cloned.1.call-update) | async-done | bytes 1048592 | tf_op jit(solution)/shard_map/psum | solution.py:125
  (125 shorter events, 75.1 us)
Async XLA Ops:
  8.0 7.3 %copy-start.30 = (f32[2048,128]{1,0:T(8,128)S(1)}, f32[2048,128]{1,0:T(8,128)}, u32[]{:S(2)}) copy-start(f32[2048,128]{1,0:T(8,128)} %param.3) | copy-start | bytes 3145732
  8.0 590.2 %all-reduce.3.cloned.1.call-start = ((), (), s32[]{:S(2)}) async-start(), calls=%async_computation.2 | async-start | bytes 2097152 | tf_op jit(solution)/shard_map/psum | solution.py:125
  46.9 4.9 copy-start.6
  46.9 5.9 copy-start.16
  67.3 3.5 copy-start.17
  67.3 4.7 copy-start.7
  72.0 2.2 copy-start.1
  74.2 2.2 copy-start.11
  154.8 3.5 copy-start.2
  158.2 5.8 copy-start.8
  158.2 7.1 %copy-start.12 = (f32[512,2048]{1,0:T(8,128)S(1)}, f32[512,2048]{1,0:T(8,128)}, u32[]{:S(2)}) copy-start(f32[512,2048]{1,0:T(8,128)} %get-tuple-element.58) | copy-start | bytes 12582916
  193.2 3.5 copy-start.18
  193.3 4.7 copy-start.9
  198.0 2.2 copy-start.3
  200.2 2.2 copy-start.13
  202.3 75.3 %copy-start.29 = (f32[2048,128]{1,0:T(8,128)S(1)}, f32[2048,128]{1,0:T(8,128)}, u32[]{:S(2)}) copy-start(f32[2048,128]{1,0:T(8,128)} %param.5) | copy-start | bytes 3145732
  277.7 7.5 %copy-start.4 = (f32[512,2048]{1,0:T(8,128)S(1)}, f32[512,2048]{1,0:T(8,128)}, u32[]{:S(2)}) copy-start(f32[512,2048]{1,0:T(8,128)} %get-tuple-element.60) | copy-start | bytes 12582916
  285.2 5.8 copy-start.14
  291.0 5.8 copy-start.19
  340.8 7.8 %copy-start.20 = (f32[512,2048]{1,0:T(8,128)S(1)}, f32[512,2048]{1,0:T(8,128)}, u32[]{:S(2)}) copy-start(f32[512,2048]{1,0:T(8,128)} %get-tuple-element.64) | copy-start | bytes 12582916
  443.7 13.6 %copy-start.31 = (f32[2048,128]{1,0:T(8,128)S(1)}, f32[2048,128]{1,0:T(8,128)}, u32[]{:S(2)}) copy-start(f32[2048,128]{1,0:T(8,128)} %param.3) | copy-start | bytes 3145732
  455.2 52.9 %copy-start.21 = (f32[512,2048]{1,0:T(8,128)}, f32[512,2048]{1,0:T(8,128)S(1)}, u32[]{:S(2)}) copy-start(f32[512,2048]{1,0:T(8,128)S(1)} %get-tuple-element.38) | copy-start | bytes 12582916
  455.2 8.8 %copy-start.10 = (f32[512,2048]{1,0:T(8,128)S(1)}, f32[512,2048]{1,0:T(8,128)}, u32[]{:S(2)}) copy-start(f32[512,2048]{1,0:T(8,128)} %get-tuple-element.62) | copy-start | bytes 12582916
  464.0 7.2 %copy-start.5 = (f32[512,2048]{1,0:T(8,128)S(1)}, f32[512,2048]{1,0:T(8,128)}, u32[]{:S(2)}) copy-start(f32[512,2048]{1,0:T(8,128)} %get-tuple-element.60) | copy-start | bytes 12582916
  471.3 7.1 %copy-start.15 = (f32[512,2048]{1,0:T(8,128)S(1)}, f32[512,2048]{1,0:T(8,128)}, u32[]{:S(2)}) copy-start(f32[512,2048]{1,0:T(8,128)} %get-tuple-element.58) | copy-start | bytes 12582916
  471.3 14.4 %copy-start.28 = (f32[512,2048]{1,0:T(8,128)S(1)}, f32[512,2048]{1,0:T(8,128)}, u32[]{:S(2)}) copy-start(f32[512,2048]{1,0:T(8,128)} %get-tuple-element.66) | copy-start | bytes 12582916
  478.3 7.4 %copy-start.27 = (f32[512,2048]{1,0:T(8,128)S(1)}, f32[512,2048]{1,0:T(8,128)}, u32[]{:S(2)}) copy-start(f32[512,2048]{1,0:T(8,128)} %get-tuple-element.67) | copy-start | bytes 12582916
  494.1 14.0 %copy-start.25 = (f32[512,2048]{1,0:T(8,128)}, f32[512,2048]{1,0:T(8,128)S(1)}, u32[]{:S(2)}) copy-start(f32[512,2048]{1,0:T(8,128)S(1)} %get-tuple-element.40) | copy-start | bytes 12582916
  494.1 14.0 %copy-start.26 = (f32[512,2048]{1,0:T(8,128)}, f32[512,2048]{1,0:T(8,128)S(1)}, u32[]{:S(2)}) copy-start(f32[512,2048]{1,0:T(8,128)S(1)} %get-tuple-element.39) | copy-start | bytes 12582916
  515.9 82.4 %reduce-scatter.2.cloned.1.call-start = ((), (), s32[]{:S(2)}) async-start(), calls=%async_computation.1 | async-start | bytes 1179648 | tf_op jit(solution)/shard_map/reduce_scatter | solution.py:124
  515.9 11.0 %copy-start.24 = (f32[512,2048]{1,0:T(8,128)S(1)}, f32[512,2048]{1,0:T(8,128)}, u32[]{:S(2)}) copy-start(f32[512,2048]{1,0:T(8,128)} %copy-done.23) | copy-start | bytes 12582916
  521.5 8.9 %copy-start.22 = (f32[512,2048]{1,0:T(8,128)S(1)}, f32[512,2048]{1,0:T(8,128)}, u32[]{:S(2)}) copy-start(f32[512,2048]{1,0:T(8,128)} %copy-done.21) | copy-start | bytes 12582916
  (2 other events, 3.4 us)
Sparse Core Ops, SparseCore 0:
  516.0 82.1 all-reduce.2
Sparse Core Ops, SparseCore 1:
  535.0 27.4 reduce-scatter.1
where the time goes:
time: 615 us; the launch traced here: 608 us
  blocking collectives  316 us (51%)
  matrix products  121 us (20%)
  other arithmetic  75.4 us (12%)
  waiting for transfers between devices  63.3 us (10%)
  between operations  16.5 us (3%)
  local copies, waits for them, and re-layouts  15.4 us (3%)
    pmax x2, blocking collectives, col_global(): top = lax.pmax(peak, 'pt')  79.3 us
    psum x2, blocking collectives, col_global(): total = lax.psum(total * jnp.exp(peak - top), 'pt')  71.9 us
    psum x1, waiting for transfers between devices, per_device(): centroid_grad_out = lax.psum(direct + rest, 'pt')  63.3 us
    psum x1, blocking collectives, per_device(): lax.psum(col_edge, 'pt')  38.2 us
    psum x1, blocking collectives, per_device(): dg1 = lax.psum(col_back, 'pt')  36 us
    pmax x2, blocking collectives, row_global(): top = lax.pmax(peak, 'ct')  28.9 us
    dot_general x4, matrix products, per_device(): direct = direct + jnp.einsum('ij,id->jd', plan, cot, precision=highest)  28.5 us
    dot_general x4, matrix products, per_device(): jnp.einsum('ij,id->jd', dz, block_rows, precision=highest)  28.4 us
  transfers between devices with their start and end apart: 2, of which 1 were waited for; matrix products, arithmetic and copies ran while one was open for 3% of the time, Pallas kernels for 0%

commit v1 on v0

v1 whole, which is shorter than its diff:
```python
import functools
import math

import jax
import jax.numpy as jnp
from jax import lax
from jax.experimental import pallas as pl
from jax.experimental.pallas import tpu as pltpu
from jax.sharding import PartitionSpec as P

L = 128
F32 = jnp.float32
BF16 = jnp.bfloat16
VMEM_LIMIT = 20 * 1024 * 1024


def split(x):
    high = x.astype(BF16)
    return high, (x - high.astype(F32)).astype(BF16)


def spread(vec_ref, index):
    return jnp.broadcast_to(vec_ref[pl.ds(index, 1), :], (L, L)).T


def fold_rows(tile):
    return jnp.sum(tile.T, axis=0, keepdims=True)


def fold_sub(tile, op):
    return op(tile.reshape(L // 8, 8, L), axis=0)


def cols_of(c):
    return slice(c * L, (c + 1) * L)


def rows_of(r):
    return pl.ds(pl.multiple_of(r * L, L), L)


def send(out_ref, lead, value):
    for n in range(out_ref.shape[0]):
        out_ref[(n,) + lead] = value


def copies(out_ref):
    for n in range(1, out_ref.shape[0]):
        out_ref[n] = out_ref[0]


def product(left_ref, right_ref, out_ref, a_ref, b_ref, scale):
    high, low = split(left_ref[...] * scale)
    for k, part in enumerate((high, high, low, low)):
        a_ref[:, cols_of(k)] = part
    high, low = split(right_ref[...])
    for k, part in enumerate((high, low, high, low)):
        b_ref[:, cols_of(k)] = part
    rows, cols = out_ref.shape
    tile = min(256, cols)
    chunk = min(512, rows)

    def body(step, carry):
        c = step // (rows // chunk)
        r = step % (rows // chunk)
        rs = pl.ds(pl.multiple_of(r * chunk, chunk), chunk)
        cs = pl.ds(pl.multiple_of(c * tile, tile), tile)
        out_ref[rs, cs] = lax.dot_general(
            a_ref[rs, :], b_ref[cs, :], (((1,), (1,)), ((), ())), preferred_element_type=F32
        )
        return carry

    lax.fori_loop(0, (cols // tile) * (rows // chunk), body, 0)


def scores_kernel(scale, p_ref, c_ref, z_ref, stat_ref, a_ref, b_ref):
    product(p_ref, c_ref, z_ref, a_ref, b_ref, scale)
    nr, nc = z_ref.shape[0] // L, z_ref.shape[1] // L

    def body(r, carry):
        rs = rows_of(r)
        top = z_ref[rs, cols_of(0)]
        for c in range(1, nc):
            top = jnp.maximum(top, z_ref[rs, cols_of(c)])
        peak = jnp.max(top.T, axis=0, keepdims=True)
        wide = jnp.broadcast_to(peak, (L, L)).T
        total = jnp.zeros((L, L), F32)
        for c in range(nc):
            total = total + jnp.exp(z_ref[rs, cols_of(c)] - wide)
        stat_ref[0, 0, pl.ds(r, 1), :] = peak
        stat_ref[0, 1, pl.ds(r, 1), :] = fold_rows(total)
        return carry

    lax.fori_loop(0, nr, body, 0)
    copies(stat_ref)


def weights_kernel(cot_ref, c_ref, w_ref, a_ref, b_ref):
    product(cot_ref, c_ref, w_ref, a_ref, b_ref, 1.0)


def merged(stat_ref):
    peak = stat_ref[0, 0]
    for n in range(1, stat_ref.shape[0]):
        peak = jnp.maximum(peak, stat_ref[n, 0])
    total = jnp.zeros_like(peak)
    for n in range(stat_ref.shape[0]):
        total = total + stat_ref[n, 1] * jnp.exp(stat_ref[n, 0] - peak)
    return peak + jnp.log(total)


def summed(ref, *lead):
    total = ref[(0,) + lead]
    for n in range(1, ref.shape[0]):
        total = total + ref[(n,) + lead]
    return total


def cols_kernel(z_ref, rowstat_ref, stat_ref, f1_ref, peak_ref, total_ref):
    nr, nc = z_ref.shape[0] // L, z_ref.shape[1] // L
    f1_ref[...] = -merged(rowstat_ref)
    peak_ref[...] = jnp.full_like(peak_ref, -jnp.inf)
    total_ref[...] = jnp.zeros_like(total_ref)

    def body(r, carry):
        rs = rows_of(r)
        shift = spread(f1_ref, r)
        for c in range(nc):
            cs = cols_of(c)
            shifted = z_ref[rs, cs] + shift
            old = peak_ref[:, cs]
            new = jnp.maximum(old, fold_sub(shifted, jnp.max))
            terms = jnp.exp(shifted.reshape(L // 8, 8, L) - new[None])
            total_ref[:, cs] = total_ref[:, cs] * jnp.exp(old - new) + jnp.sum(terms, axis=0)
            peak_ref[:, cs] = new
        return carry

    lax.fori_loop(0, nr, body, 0)
    for c in range(nc):
        cs = cols_of(c)
        peak = jnp.max(peak_ref[:, cs], axis=0, keepdims=True)
        total = jnp.sum(total_ref[:, cs] * jnp.exp(peak_ref[:, cs] - peak), axis=0, keepdims=True)
        stat_ref[0, 0, c : c + 1, :] = peak
        stat_ref[0, 1, c : c + 1, :] = total
    copies(stat_ref)


def plan_kernel(z_ref, colstat_ref, f1_ref, b_ref, sum_ref, s_ref, shift_ref):
    nr, nc = z_ref.shape[0] // L, z_ref.shape[1] // L
    lse = merged(colstat_ref)
    shift_ref[...] = -lse
    s_ref[...] = jnp.exp(lse)

    def body(r, carry):
        rs = rows_of(r)
        shift = spread(f1_ref, r)
        total = jnp.zeros((L, L), F32)
        for c in range(nc):
            cs = cols_of(c)
            value = jnp.exp((z_ref[rs, cs] + shift) + shift_ref[c : c + 1, :])
            b_ref[rs, cs] = value
            total = total + value
        sum_ref[0, pl.ds(r, 1), :] = fold_rows(total)
        return carry

    lax.fori_loop(0, nr, body, 0)
    copies(sum_ref)


def edges_kernel(b_ref, w_ref, rowsum_ref, stat_ref, ib_ref, one_ref, two_ref):
    nr, nc = b_ref.shape[0] // L, b_ref.shape[1] // L
    ib_ref[...] = 1.0 / summed(rowsum_ref)
    one_ref[...] = jnp.zeros_like(one_ref)
    two_ref[...] = jnp.zeros_like(two_ref)

    def body(r, carry):
        rs = rows_of(r)
        inv = spread(ib_ref, r)
        for c in range(nc):
            cs = cols_of(c)
            value = b_ref[rs, cs] * inv
            one_ref[:, cs] += fold_sub(value, jnp.sum)
            two_ref[:, cs] += fold_sub(value * w_ref[rs, cs], jnp.sum)
        return carry

    lax.fori_loop(0, nr, body, 0)
    for c in range(nc):
        cs = cols_of(c)
        stat_ref[0, 0, c : c + 1, :] = jnp.sum(one_ref[:, cs], axis=0, keepdims=True)
        stat_ref[0, 1, c : c + 1, :] = jnp.sum(two_ref[:, cs], axis=0, keepdims=True)
    copies(stat_ref)


def rowback_kernel(share, ratio, b_ref, w_ref, colsum_ref, g_ref, sum_ref, q_ref, h_ref):
    nr, nc = b_ref.shape[0] // L, b_ref.shape[1] // L
    q = share / summed(colsum_ref, 0)
    q_ref[...] = q
    h_ref[...] = ratio * (q * summed(colsum_ref, 1))

    def body(r, carry):
        rs = rows_of(r)
        total = jnp.zeros((L, L), F32)
        for c in range(nc):
            cs = cols_of(c)
            value = (b_ref[rs, cs] * q_ref[c : c + 1, :]) * (w_ref[rs, cs] - h_ref[c : c + 1, :])
            g_ref[rs, cs] = value
            total = total + value
        sum_ref[0, pl.ds(r, 1), :] = fold_rows(total)
        return carry

    lax.fori_loop(0, nr, body, 0)
    copies(sum_ref)


def colback_kernel(b_ref, rowsum_ref, ib_ref, sum_ref, y_ref, acc_ref):
    nr, nc = b_ref.shape[0] // L, b_ref.shape[1] // L
    y_ref[...] = (summed(rowsum_ref) * ib_ref[...]) * ib_ref[...]
    acc_ref[...] = jnp.zeros_like(acc_ref)

    def body(r, carry):
        rs = rows_of(r)
        y = spread(y_ref, r)
        for c in range(nc):
            cs = cols_of(c)
            acc_ref[:, cs] += fold_sub(b_ref[rs, cs] * y, jnp.sum)
        return carry

    lax.fori_loop(0, nr, body, 0)
    for c in range(nc):
        sum_ref[0, c : c + 1, :] = -jnp.sum(acc_ref[:, cols_of(c)], axis=0, keepdims=True)
    copies(sum_ref)


def lastrow_kernel(b_ref, colsum_ref, sum_ref, d_ref):
    nr, nc = b_ref.shape[0] // L, b_ref.shape[1] // L
    d_ref[...] = summed(colsum_ref)

    def body(r, carry):
        rs = rows_of(r)
        total = jnp.zeros((L, L), F32)
        for c in range(nc):
            total = total + b_ref[rs, cols_of(c)] * d_ref[c : c + 1, :]
        sum_ref[0, pl.ds(r, 1), :] = -fold_rows(total)
        return carry

    lax.fori_loop(0, nr, body, 0)
    copies(sum_ref)


def grads_kernel(
    scale, b_ref, g_ref, rowsum_ref, d_ref, y_ref, ib_ref, s_ref, q_ref, p_ref, c_ref, cot_ref,
    pg_ref, cg_ref, f_ref, pt_ref, ct_ref, cc_ref, dz_ref, bb_ref, one_ref, two_ref
):
    rows, cols = b_ref.shape
    nr, nc = rows // L, cols // L
    f_ref[...] = summed(rowsum_ref)
    high, low = split(c_ref[...] * scale)
    cc_ref[:, :L] = high
    cc_ref[:, L:] = low
    for r in range(nr):
        rs = slice(r * L, (r + 1) * L)
        high, low = split((p_ref[rs, :] * scale).T)
        pt_ref[:L, rs] = high
        pt_ref[L:, rs] = low
        high, low = split(cot_ref[rs, :].T * ib_ref[r : r + 1, :])
        ct_ref[:L, rs] = high
        ct_ref[L:, rs] = low
    one_ref[...] = jnp.zeros_like(one_ref)
    two_ref[...] = jnp.zeros_like(two_ref)
    chunk = min(256, rows)
    part = min(512, cols)

    def body(k, carry):
        for sub in range(chunk // L):
            r = k * (chunk // L) + sub
            rs = rows_of(r)
            inv, y, f = spread(ib_ref, r), spread(y_ref, r), spread(f_ref, r)
            here = slice(sub * L, (sub + 1) * L)
            there = slice(chunk + sub * L, chunk + (sub + 1) * L)
            for c in range(nc):
                cs = cols_of(c)
                base = b_ref[rs, cs]
                factor = (y + d_ref[c : c + 1, :]) + s_ref[c : c + 1, :] * f
                high, low = split(g_ref[rs, cs] * inv - base * factor)
                dz_ref[here, cs] = high
                dz_ref[there, cs] = low
                high, low = split(base)
                bb_ref[here, cs] = high
                bb_ref[there, cs] = low
        ks = pl.ds(pl.multiple_of(k * chunk, chunk), chunk)
        both = jnp.dot(dz_ref[...], cc_ref[...], preferred_element_type=F32)
        both = both[:, :L] + both[:, L:]
        pg_ref[ks, :] = both[:chunk] + both[chunk:]
        for n in range(cols // part):
            ns = slice(n * part, (n + 1) * part)
            for left, right, acc in ((pt_ref, dz_ref, one_ref), (ct_ref, bb_ref, two_ref)):
                lhs = left[:, ks]
                acc[:, ns] += jnp.dot(lhs, right[:chunk, ns], preferred_element_type=F32) + jnp.dot(
                    lhs, right[chunk:, ns], preferred_element_type=F32
                )
        return carry

    lax.fori_loop(0, rows // chunk, body, 0)
    for c in range(nc):
        cs = cols_of(c)
        plan = (two_ref[:L, cs] + two_ref[L:, cs]) * q_ref[c : c + 1, :]
        cg_ref[cs, :] = ((one_ref[:L, cs] + one_ref[L:, cs]) + plan).T


def call(kernel, name, outs, scratch, args, aliases=None, flops=0):
    big = lambda a: a.ndim == 2 and a.shape[0] >= 256 and a.shape[1] >= 256
    shapes = [
        pltpu.VMEM(o, F32) if len(o) == 2 and min(o) >= 256 else jax.ShapeDtypeStruct(o, F32)
        for o in outs
    ]
    args = [pltpu.with_memory_space_constraint(a, pltpu.VMEM) if big(a) else a for a in args]
    whole = pl.BlockSpec(memory_space=pltpu.VMEM)
    return pl.pallas_call(
        kernel,
        name=name,
        out_shape=shapes,
        in_specs=[whole] * len(args),
        out_specs=[whole] * len(outs),
        scratch_shapes=[pltpu.VMEM(s, t) for s, t in scratch],
        input_output_aliases=aliases or {},
        compiler_params=pltpu.CompilerParams(vmem_limit_bytes=VMEM_LIMIT),
        cost_estimate=pl.CostEstimate(flops=flops, bytes_accessed=1 << 20, transcendentals=0),
    )(*args)


def per_device(points, centroids, cotangent):
    rows, width = points.shape
    cols = centroids.shape[0]
    npt, nct = lax.axis_size("pt"), lax.axis_size("ct")
    share = (rows * npt) / (cols * nct)
    ratio = (cols * nct) / (rows * npt)
    scale = 3.0 / math.sqrt(width)
    nr, nc = rows // L, cols // L

    def over(axis, value):
        return lax.all_to_all(value, axis, 0, 0, tiled=True)

    big = (rows, cols)
    rvec, cvec = (nr, L), (nc, L)
    tall = [((rows, 4 * L), BF16), ((cols, 4 * L), BF16)]
    strip = ((8, cols), F32)
    z, stat = call(
        functools.partial(scores_kernel, scale), "scores", [big, (nct, 2) + rvec], tall,
        [points, centroids], flops=8 * rows * cols * L,
    )
    stat = over("ct", stat)
    (w,) = call(weights_kernel, "weights", [big], tall, [cotangent, centroids], flops=8 * rows * cols * L)
    stat, f1 = call(cols_kernel, "cols", [(npt, 2) + cvec, rvec], [strip, strip], [z, stat])
    stat = over("pt", stat)
    b, sums, s = call(
        plan_kernel, "plan", [big, (nct,) + rvec, cvec], [(cvec, F32)], [z, stat, f1], {0: 0}
    )
    sums = over("ct", sums)
    stat, ib = call(edges_kernel, "edges", [(npt, 2) + cvec, rvec], [strip, strip], [b, w, sums])
    stat = over("pt", stat)
    g, sums, q = call(
        functools.partial(rowback_kernel, share, ratio), "rowback",
        [big, (nct,) + rvec, cvec], [(cvec, F32)], [b, w, stat], {1: 0},
    )
    sums = over("ct", sums)
    sums, y = call(colback_kernel, "colback", [(npt,) + cvec, rvec], [strip], [b, sums, ib])
    sums = over("pt", sums)
    sums, d = call(lastrow_kernel, "lastrow", [(nct,) + rvec, cvec], [], [b, sums])
    sums = over("ct", sums)
    chunk = min(256, rows)
    pg, cg = call(
        functools.partial(grads_kernel, scale), "grads", [(rows, width), (cols, width)],
        [
            (rvec, F32), ((2 * L, rows), BF16), ((2 * L, rows), BF16), ((cols, 2 * L), BF16),
            ((2 * chunk, cols), BF16), ((2 * chunk, cols), BF16),
            ((2 * L, cols), F32), ((2 * L, cols), F32),
        ],
        [b, g, sums, d, y, ib, s, q, points, centroids, cotangent],
        flops=24 * rows * cols * L,
    )
    cg = over("pt", cg.reshape(npt, cols // npt, width))
    pg = over("ct", pg.reshape(nct, rows // nct, width))
    cg = jnp.sum(cg, axis=0)
    point_grad = jnp.sum(pg, axis=0)
    cg = over("pt", jnp.broadcast_to(cg[None], (npt, cols // npt, width)))
    return (point_grad, cg.reshape(cols, width))


def solution(mesh):
    return jax.shard_map(
        per_device,
        mesh=mesh,
        in_specs=(P("pt", None), P("ct", None), P("pt", None)),
        out_specs=(P(("pt", "ct"), None), P("ct", None)),
        check_vma=False,
    )
```

time: 615 us -> 256 us (0.42)
  blocking collectives: 316 us -> 88.9 us
  matrix products: 121 us -> 0 us
  Pallas kernels: 0 us -> 81.9 us
  other arithmetic: 75.4 us -> 0.77 us
  waiting for transfers between devices: 63.3 us -> 32.8 us
  local copies, waits for them, and re-layouts: 15.4 us -> 39 us
  between operations: 16.5 us -> 0.75 us
  starting transfers between devices: 0.08 us -> 10.6 us
    psum x8 -> x0, blocking collectives: 208 us -> none  [the longest x2 71.9 us: col_global(): total = lax.psum(total * jnp.exp(peak - top), 'pt')]
    dot_general x20 -> x0, matrix products: 121 us -> none  [the longest x4 28.5 us: per_device(): direct = direct + jnp.einsum('ij,id->jd', plan, cot, precision=highest)]
    pmax x4 -> x0, blocking collectives: 108 us -> none  [the longest x2 79.3 us: col_global(): top = lax.pmax(peak, 'pt')]
    all_to_all x0 -> x7, blocking collectives: none -> 88.9 us  [over(): return lax.all_to_all(value, axis, 0, 0, tiled=True)]
    pallas_call x0 -> x9, Pallas kernels: none -> 81.9 us  [call(): pl.pallas_call(kernel, name=name, out_shape=shapes, in_specs=[whole] * le...]
    psum x1 -> x0, waiting for transfers between devices: 63.3 us -> none  [per_device(): centroid_grad_out = lax.psum(direct + rest, 'pt')]
    reduce_sum x15 -> x2, other arithmetic: 44.1 us -> 0.77 us  [the longest x1 0.71 us: per_device(): point_grad = jnp.sum(pg, axis=0)]
    all_to_all x0 -> x3, waiting for transfers between devices: none -> 32.8 us  [over(): return lax.all_to_all(value, axis, 0, 0, tiled=True)]
  transfers between devices with their start and end apart: 2 -> 3, of which waited for: 1 -> 2; matrix products, arithmetic and copies ran while one was open for 3% -> 0% of each run, Pallas kernels for 0% -> 4%
where the time goes in v1:
time: 256 us; the launch traced here: 255 us
  blocking collectives  88.9 us (35%)
  Pallas kernels  81.9 us (32%)
  local copies, waits for them, and re-layouts  39 us (15%)
  waiting for transfers between devices  32.8 us (13%)
  starting transfers between devices  10.6 us (4%)
    all_to_all x7, blocking collectives, over(): return lax.all_to_all(value, axis, 0, 0, tiled=True)  88.9 us
    pallas_call x9, Pallas kernels, call(): pl.pallas_call(kernel, name=name, out_shape=shapes, in_specs=[whole] * le...  81.9 us
    unnamed x21, local copies, waits for them, and re-layouts  37.9 us
    all_to_all x3, waiting for transfers between devices, over(): return lax.all_to_all(value, axis, 0, 0, tiled=True)  32.8 us
    all_to_all x3, starting transfers between devices, over(): return lax.all_to_all(value, axis, 0, 0, tiled=True)  10.6 us
  transfers between devices with their start and end apart: 3, of which 2 were waited for; matrix products, arithmetic and copies ran while one was open for 0% of the time, Pallas kernels for 4%

profile of v1, /device:TPU:0, one launch (start us, length us, event | category | flops | bytes accessed | tf_op | source)
XLA Modules:
  0.0 254.8 jit_solution(8036929019103178086)
XLA Ops:
  0.6 1.2 copy-done.6
  1.9 1.2 copy-done.9
  3.1 18.2 %scores.1 = (f32[2048,2048]{1,0:T(8,128)S(1)}, f32[8,2,16,128]{3,2,1,0:T(8,128)S(1)}) custom-call(f32[2048,128]{1,0:T(8,128)S(1)} %copy-done.9, f32[2048,128]{1,0:T(8,128)S(1)} %copy-done.6), custom_call_target="tpu_custom_call" | custom-call | flops 4294967296 | bytes 1048576 | tf_op jit(solution)/shard_map/scores/pallas_call | solution.py:318
  21.3 11.1 %all_to_all.50.rowstat_ref = f32[8,2,16,128]{3,2,1,0:T(8,128)S(1)} all-to-all(f32[8,2,16,128]{3,2,1,0:T(8,128)S(1)} %get-tuple-element.21), channel_id=1, replica_groups=mesh['pt'=16,'ct'=8] {'ct'}, dimensions={0} | all-to-all | bytes 262144 | tf_op jit(solution)/shard_map/all_to_all | solution.py:341
  32.4 4.9 %cols.1 = (f32[16,2,16,128]{3,2,1,0:T(8,128)S(1)}, f32[16,128]{1,0:T(8,128)S(1)}) custom-call(f32[2048,2048]{1,0:T(8,128)S(1)} %get-tuple-element.20.z_ref, f32[8,2,16,128]{3,2,1,0:T(8,128)S(1)} %all_to_all.50.rowstat_ref), custom_call_target="tpu_custom_call" | custom-call | bytes 1048576 | tf_op jit(solution)/shard_map/cols/pallas_call | solution.py:318
  37.3 15.8 %all_to_all.51.colstat_ref = f32[16,2,16,128]{3,2,1,0:T(8,128)S(1)} all-to-all(f32[16,2,16,128]{3,2,1,0:T(8,128)S(1)} %get-tuple-element.22), channel_id=1, replica_groups=mesh['pt'=16,'ct'=8] {'pt'}, dimensions={0} | all-to-all | bytes 524288 | tf_op jit(solution)/shard_map/all_to_all | solution.py:341
  53.1 8.8 %plan.1 = (f32[2048,2048]{1,0:T(8,128)S(1)}, f32[8,16,128]{2,1,0:T(8,128)}, f32[16,128]{1,0:T(8,128)S(1)}) custom-call(f32[2048,2048]{1,0:T(8,128)S(1)} %get-tuple-element.20.z_ref, f32[16,2,16,128]{3,2,1,0:T(8,128)S(1)} %all_to_all.51.colstat_ref, f32[16,128]{1,0:T(8,128)S(1)} %get-tuple-element.23.f1_ref), custom_call_target="tpu_custom_call", output_to_operand_aliasing={{0}: (0, {})} | custom-call | bytes 1048576 | tf_op jit(solution)/shard_map/plan/pallas_call | solution.py:318
  61.9 5.7 %copy-done = f32[2048,2048]{1,0:T(8,128)} copy-done((f32[2048,2048]{1,0:T(8,128)}, f32[2048,2048]{1,0:T(8,128)S(1)}, u32[]{:S(2)}) %copy-start) | copy-done | bytes 16777240
  67.6 3.4 %all-to-all-start.2 = ((f32[8,16,128]{2,1,0:T(8,128)}), f32[8,16,128]{2,1,0:T(8,128)S(1)}, u32[]{:S(2)}, u32[]{:S(2)}) async-start(f32[8,16,128]{2,1,0:T(8,128)} %get-tuple-element.25), calls=%async_computation.2 | async-start | bytes 131072 | tf_op jit(solution)/shard_map/all_to_all | solution.py:341
  71.0 11.1 %weights.1.w_ref = f32[2048,2048]{1,0:T(8,128)S(1)} custom-call(f32[2048,128]{1,0:T(8,128)S(1)} %copy-done.8, f32[2048,128]{1,0:T(8,128)S(1)} %copy-done.7), custom_call_target="tpu_custom_call" | custom-call | flops 4294967296 | bytes 1048576 | tf_op jit(solution)/shard_map/weights/pallas_call | solution.py:318
  82.1 5.7 %copy-done.2 = f32[2048,2048]{1,0:T(8,128)} copy-done((f32[2048,2048]{1,0:T(8,128)}, f32[2048,2048]{1,0:T(8,128)S(1)}, u32[]{:S(2)}) %copy-start.2) | copy-done | bytes 16777240
  87.8 5.8 %copy-done.1 = f32[2048,2048]{1,0:T(8,128)S(1)} copy-done((f32[2048,2048]{1,0:T(8,128)S(1)}, f32[2048,2048]{1,0:T(8,128)}, u32[]{:S(2)}) %copy-start.1) | copy-done | bytes 16777240
  93.6 5.8 %copy-done.3 = f32[2048,2048]{1,0:T(8,128)S(1)} copy-done((f32[2048,2048]{1,0:T(8,128)S(1)}, f32[2048,2048]{1,0:T(8,128)}, u32[]{:S(2)}) %copy-start.3) | copy-done | bytes 16777240
  99.3 3.4 %edges.1 = (f32[16,2,16,128]{3,2,1,0:T(8,128)S(1)}, f32[16,128]{1,0:T(8,128)S(1)}) custom-call(f32[2048,2048]{1,0:T(8,128)S(1)} %copy-done.1, f32[2048,2048]{1,0:T(8,128)S(1)} %copy-done.3, f32[8,16,128]{2,1,0:T(8,128)S(1)} %all-to-all-done.2.rowsum_ref), custom_call_target="tpu_custom_call" | custom-call | bytes 1048576 | tf_op jit(solution)/shard_map/edges/pallas_call | solution.py:318
  102.8 12.2 %all_to_all.52.colsum_ref = f32[16,2,16,128]{3,2,1,0:T(8,128)S(1)} all-to-all(f32[16,2,16,128]{3,2,1,0:T(8,128)S(1)} %get-tuple-element.26), channel_id=1, replica_groups=mesh['pt'=16,'ct'=8] {'pt'}, dimensions={0} | all-to-all | bytes 524288 | tf_op jit(solution)/shard_map/all_to_all | solution.py:341
  115.0 6.1 %rowback.1 = (f32[2048,2048]{1,0:T(8,128)S(1)}, f32[8,16,128]{2,1,0:T(8,128)S(1)}, f32[16,128]{1,0:T(8,128)S(1)}) custom-call(f32[2048,2048]{1,0:T(8,128)S(1)} %copy-done.1, f32[2048,2048]{1,0:T(8,128)S(1)} %copy-done.3, f32[16,2,16,128]{3,2,1,0:T(8,128)S(1)} %all_to_all.52.colsum_ref), custom_call_target="tpu_custom_call", output_to_operand_aliasing={{0}: (1, {})} | custom-call | bytes 1048576 | tf_op jit(solution)/shard_map/rowback/pallas_call | solution.py:318
  121.1 5.7 %copy-done.4 = f32[2048,2048]{1,0:T(8,128)} copy-done((f32[2048,2048]{1,0:T(8,128)}, f32[2048,2048]{1,0:T(8,128)S(1)}, u32[]{:S(2)}) %copy-start.4) | copy-done | bytes 16777240
  126.8 10.0 %all_to_all.53.rowsum_ref = f32[8,16,128]{2,1,0:T(8,128)S(1)} all-to-all(f32[8,16,128]{2,1,0:T(8,128)S(1)} %get-tuple-element.28), channel_id=1, replica_groups=mesh['pt'=16,'ct'=8] {'ct'}, dimensions={0} | all-to-all | bytes 131072 | tf_op jit(solution)/shard_map/all_to_all | solution.py:341
  136.8 2.3 colback.1
  139.2 10.9 %all_to_all.54.colsum_ref = f32[16,16,128]{2,1,0:T(8,128)S(1)} all-to-all(f32[16,16,128]{2,1,0:T(8,128)S(1)} %get-tuple-element.30), channel_id=1, replica_groups=mesh['pt'=16,'ct'=8] {'pt'}, dimensions={0} | all-to-all | bytes 262144 | tf_op jit(solution)/shard_map/all_to_all | solution.py:341
  150.0 2.5 lastrow.1
  152.5 8.0 %all_to_all.55.rowsum_ref = f32[8,16,128]{2,1,0:T(8,128)S(1)} all-to-all(f32[8,16,128]{2,1,0:T(8,128)S(1)} %get-tuple-element.31), channel_id=1, replica_groups=mesh['pt'=16,'ct'=8] {'ct'}, dimensions={0} | all-to-all | bytes 131072 | tf_op jit(solution)/shard_map/all_to_all | solution.py:341
  160.5 5.8 %copy-done.5 = f32[2048,2048]{1,0:T(8,128)S(1)} copy-done((f32[2048,2048]{1,0:T(8,128)S(1)}, f32[2048,2048]{1,0:T(8,128)}, u32[]{:S(2)}) %copy-start.5) | copy-done | bytes 16777240
  166.3 24.7 %grads.1 = (f32[2048,128]{1,0:T(8,128)}, f32[2048,128]{1,0:T(8,128)}) custom-call(f32[2048,2048]{1,0:T(8,128)S(1)} %copy-done.1, f32[2048,2048]{1,0:T(8,128)S(1)} %copy-done.5, f32[8,16,128]{2,1,0:T(8,128)S(1)} %all_to_all.55.rowsum_ref, f32[16,128]{1,0:T(8,128)S(1)} %get-tuple-element.32.d_ref, f32[16,128]{1,0:T(8,128)S(1)} %get-tuple-element.33.y_ref, ...), custom_call_target="tpu_custom_call" | custom-call | flops 12884901888 | bytes 1048576 | tf_op jit(solution)/shard_map/grads/pallas_call | solution.py:318
  191.0 20.9 %all_to_all.56 = f32[16,128,128]{2,1,0:T(8,128)S(1)} all-to-all(f32[16,128,128]{2,1,0:T(8,128)} %bitcast.4), channel_id=1, replica_groups=mesh['pt'=16,'ct'=8] {'pt'}, dimensions={0} | all-to-all | bytes 2097152 | tf_op jit(solution)/shard_map/all_to_all | solution.py:341
  211.9 3.6 %all-to-all-start.7 = ((f32[8,256,128]{2,1,0:T(8,128)}), f32[8,256,128]{2,1,0:T(8,128)S(1)}, u32[]{:S(2)}, u32[]{:S(2)}) async-start(f32[8,256,128]{2,1,0:T(8,128)} %bitcast), calls=%async_computation.7 | async-start | bytes 2097152 | tf_op jit(solution)/shard_map/all_to_all | solution.py:341
  215.6 15.8 %all-to-all-done.7 = f32[8,256,128]{2,1,0:T(8,128)S(1)} async-done(((f32[8,256,128]{2,1,0:T(8,128)}), f32[8,256,128]{2,1,0:T(8,128)S(1)}, u32[]{:S(2)}, u32[]{:S(2)}) %all-to-all-start.7) | async-done | bytes 1048608 | tf_op jit(solution)/shard_map/all_to_all | solution.py:341
  231.4 1.1 broadcast_in_dim.2
  232.5 3.7 %all-to-all-start.9 = ((f32[16,128,128]{2,1,0:T(8,128)}), f32[16,128,128]{2,1,0:T(8,128)S(1)}, u32[]{:S(2)}, u32[]{:S(2)}) async-start(f32[16,128,128]{2,1,0:T(8,128)} %broadcast_in_dim.2), calls=%async_computation.9 | async-start | bytes 2097152 | tf_op jit(solution)/shard_map/all_to_all | solution.py:341
  236.1 0.7 reduce_sum.18
  236.8 17.0 %all-to-all-done.9 = f32[16,128,128]{2,1,0:T(8,128)S(1)} async-done(((f32[16,128,128]{2,1,0:T(8,128)}), f32[16,128,128]{2,1,0:T(8,128)S(1)}, u32[]{:S(2)}, u32[]{:S(2)}) %all-to-all-start.9) | async-done | bytes 1048608 | tf_op jit(solution)/shard_map/all_to_all | solution.py:341
  253.8 1.0 copy.10
  (14 shorter events, 0.1 us)
Async XLA Ops:
  0.6 1.2 copy-start.6
  1.9 1.2 copy-start.9
  32.4 38.6 %copy-start.7 = (f32[2048,128]{1,0:T(8,128)S(1)}, f32[2048,128]{1,0:T(8,128)}, u32[]{:S(2)}) copy-start(f32[2048,128]{1,0:T(8,128)} %c_ref.5) | copy-start | bytes 3145732
  32.4 38.6 %copy-start.8 = (f32[2048,128]{1,0:T(8,128)S(1)}, f32[2048,128]{1,0:T(8,128)}, u32[]{:S(2)}) copy-start(f32[2048,128]{1,0:T(8,128)} %cot_ref.3) | copy-start | bytes 3145732
  61.9 5.7 %copy-start = (f32[2048,2048]{1,0:T(8,128)}, f32[2048,2048]{1,0:T(8,128)S(1)}, u32[]{:S(2)}) copy-start(f32[2048,2048]{1,0:T(8,128)S(1)} %get-tuple-element.24.b_ref) | copy-start | bytes 50331652
  67.6 20.2 %all-to-all-start.2 = ((f32[8,16,128]{2,1,0:T(8,128)}), f32[8,16,128]{2,1,0:T(8,128)S(1)}, u32[]{:S(2)}, u32[]{:S(2)}) async-start(f32[8,16,128]{2,1,0:T(8,128)} %get-tuple-element.25), calls=%async_computation.2 | async-start | bytes 131072 | tf_op jit(solution)/shard_map/all_to_all | solution.py:341
  82.0 5.7 %copy-start.2 = (f32[2048,2048]{1,0:T(8,128)}, f32[2048,2048]{1,0:T(8,128)S(1)}, u32[]{:S(2)}) copy-start(f32[2048,2048]{1,0:T(8,128)S(1)} %weights.1.w_ref) | copy-start | bytes 50331652
  87.8 5.8 %copy-start.1 = (f32[2048,2048]{1,0:T(8,128)S(1)}, f32[2048,2048]{1,0:T(8,128)}, u32[]{:S(2)}) copy-start(f32[2048,2048]{1,0:T(8,128)} %copy-done) | copy-start | bytes 50331652
  93.6 5.8 %copy-start.3 = (f32[2048,2048]{1,0:T(8,128)S(1)}, f32[2048,2048]{1,0:T(8,128)}, u32[]{:S(2)}) copy-start(f32[2048,2048]{1,0:T(8,128)} %copy-done.2) | copy-start | bytes 50331652
  121.1 5.8 %copy-start.4 = (f32[2048,2048]{1,0:T(8,128)}, f32[2048,2048]{1,0:T(8,128)S(1)}, u32[]{:S(2)}) copy-start(f32[2048,2048]{1,0:T(8,128)S(1)} %get-tuple-element.27.g_ref) | copy-start | bytes 50331652
  160.5 5.8 %copy-start.5 = (f32[2048,2048]{1,0:T(8,128)S(1)}, f32[2048,2048]{1,0:T(8,128)}, u32[]{:S(2)}) copy-start(f32[2048,2048]{1,0:T(8,128)} %copy-done.4) | copy-start | bytes 50331652
  211.9 19.5 %all-to-all-start.7 = ((f32[8,256,128]{2,1,0:T(8,128)}), f32[8,256,128]{2,1,0:T(8,128)S(1)}, u32[]{:S(2)}, u32[]{:S(2)}) async-start(f32[8,256,128]{2,1,0:T(8,128)} %bitcast), calls=%async_computation.7 | async-start | bytes 2097152 | tf_op jit(solution)/shard_map/all_to_all | solution.py:341
  232.5 21.4 %all-to-all-start.9 = ((f32[16,128,128]{2,1,0:T(8,128)}), f32[16,128,128]{2,1,0:T(8,128)S(1)}, u32[]{:S(2)}, u32[]{:S(2)}) async-start(f32[16,128,128]{2,1,0:T(8,128)} %broadcast_in_dim.2), calls=%async_computation.9 | async-start | bytes 2097152 | tf_op jit(solution)/shard_map/all_to_all | solution.py:341

commit v2 on v1

v2 whole, which is shorter than its diff:
```python
import functools
import itertools
import math

import jax
import jax.numpy as jnp
from jax import lax
from jax.experimental import pallas as pl
from jax.experimental.pallas import tpu as pltpu
from jax.sharding import PartitionSpec as P

L = 128
F32 = jnp.float32
BF16 = jnp.bfloat16
ROW_UNROLL = 16
PLAN_UNROLL = 2
CHUNK = 256


def split(x):
    high = x.astype(BF16)
    return high, (x - high.astype(F32)).astype(BF16)


def spread(vec_ref, index):
    return jnp.broadcast_to(vec_ref[pl.ds(index, 1), :], (L, L)).T


def fold_rows(tile):
    return jnp.sum(tile.T, axis=0, keepdims=True)


def fold_sub(tile, op):
    return op(tile.reshape(L // 8, 8, L), axis=0)


def cols_of(c):
    return slice(c * L, (c + 1) * L)


def rows_of(r):
    if isinstance(r, int):
        return slice(r * L, (r + 1) * L)
    return pl.ds(pl.multiple_of(r * L, L), L)


def send(out_ref, lead, value):
    for n in range(out_ref.shape[0]):
        out_ref[(n,) + lead] = value


def copies(out_ref):
    for n in range(1, out_ref.shape[0]):
        out_ref[n] = out_ref[0]


def pack(left_ref, right_ref, a_ref, b_ref, scale):
    high, low = split(left_ref[...] * scale)
    for k, part in enumerate((high, high, low, low)):
        a_ref[:, cols_of(k)] = part
    high, low = split(right_ref[...])
    for k, part in enumerate((high, low, high, low)):
        b_ref[:, cols_of(k)] = part


def tiles(a_ref, b_ref, out_ref, rs, tile):
    cols = b_ref.shape[0]
    for c in range(0, cols, tile):
        out_ref[rs, c : c + tile] = lax.dot_general(
            a_ref[rs, :], b_ref[c : c + tile, :], (((1,), (1,)), ((), ())), preferred_element_type=F32
        )


def each_row(nr, body, unroll=ROW_UNROLL):
    if unroll >= nr:
        for r in range(nr):
            body(r)
        return

    def step(r, carry):
        body(r)
        return carry

    lax.fori_loop(0, nr, step, 0, unroll=min(unroll, nr))


def fetch(pairs, sem):
    moves = [pltpu.make_async_copy(src, dst, sem.at[n]) for n, (src, dst) in enumerate(pairs)]
    for move in moves:
        move.start()
    for move in moves:
        move.wait()


def planes(buf_ref):
    size = buf_ref.shape[1]
    return tuple(
        buf_ref.at[pl.ds(start, height), :]
        for start, height in ((0, size), (size, size), (2 * size, L), (2 * size + L, L))
    )


F1, S, IB, Q, H, Y, D = range(7)


def vec(buf_ref, name):
    size = buf_ref.shape[1]
    place = name % (size // L)
    return buf_ref.at[pl.ds(2 * size + 2 * L + (name // (size // L)) * (size // L), size // L), cols_of(place)]


def scores_kernel(scale, p_hbm, c_hbm, buf_ref, stat_ref, a_ref, b_ref, p_ref, c_ref, sem):
    fetch(((p_hbm, p_ref), (c_hbm, c_ref)), sem)
    pack(p_ref, c_ref, a_ref, b_ref, scale)
    z_ref = planes(buf_ref)[0]
    rows, nc = z_ref.shape[0], z_ref.shape[1] // L
    chunk = min(512, rows)
    for start in range(0, rows, chunk):
        tiles(a_ref, b_ref, z_ref, slice(start, start + chunk), min(1024, nc * L))
        for r in range(start // L, (start + chunk) // L):
            rs = slice(r * L, (r + 1) * L)
            top = z_ref[rs, cols_of(0)]
            for c in range(1, nc):
                top = jnp.maximum(top, z_ref[rs, cols_of(c)])
            peak = jnp.max(top.T, axis=0, keepdims=True)
            wide = jnp.broadcast_to(peak, (L, L)).T
            total = jnp.zeros((L, L), F32)
            for c in range(nc):
                total = total + jnp.exp(z_ref[rs, cols_of(c)] - wide)
            stat_ref[0, 0, r : r + 1, :] = peak
            stat_ref[0, 1, r : r + 1, :] = fold_rows(total)
    copies(stat_ref)


def merged(stat_ref):
    peak = stat_ref[0, 0]
    for n in range(1, stat_ref.shape[0]):
        peak = jnp.maximum(peak, stat_ref[n, 0])
    total = jnp.zeros_like(peak)
    for n in range(stat_ref.shape[0]):
        total = total + stat_ref[n, 1] * jnp.exp(stat_ref[n, 0] - peak)
    return peak + jnp.log(total)


def summed(ref, *lead):
    total = ref[(0,) + lead]
    for n in range(1, ref.shape[0]):
        total = total + ref[(n,) + lead]
    return total


def cols_kernel(
    old_ref, cot_hbm, c_hbm, rowstat_ref, buf_ref, stat_ref, peak_ref, total_ref, left_ref, right_ref,
    cot_ref, c_ref, sem
):
    fetch(((cot_hbm, cot_ref), (c_hbm, c_ref)), sem)
    b_ref = planes(old_ref)[0]
    w_ref = planes(buf_ref)[1]
    rows, cols = b_ref.shape
    nc = cols // L
    f1_ref = vec(buf_ref, F1)
    f1_ref[...] = -merged(rowstat_ref)
    peak_ref[...] = jnp.full_like(peak_ref, -jnp.inf)
    total_ref[...] = jnp.zeros_like(total_ref)
    pack(cot_ref, c_ref, left_ref, right_ref, 1.0)
    chunk = min(512, rows)
    for start in range(0, rows, chunk):
        tiles(left_ref, right_ref, w_ref, slice(start, start + chunk), min(1024, cols))
        for r in range(start // L, (start + chunk) // L):
            rs = slice(r * L, (r + 1) * L)
            shift = spread(f1_ref, r)
            for c in range(nc):
                cs = cols_of(c)
                shifted = b_ref[rs, cs] + shift
                old = peak_ref[:, cs]
                new = jnp.maximum(old, fold_sub(shifted, jnp.max))
                terms = jnp.exp(shifted.reshape(L // 8, 8, L) - new[None])
                total_ref[:, cs] = total_ref[:, cs] * jnp.exp(old - new) + jnp.sum(terms, axis=0)
                peak_ref[:, cs] = new
    for c in range(nc):
        cs = cols_of(c)
        peak = jnp.max(peak_ref[:, cs], axis=0, keepdims=True)
        total = jnp.sum(total_ref[:, cs] * jnp.exp(peak_ref[:, cs] - peak), axis=0, keepdims=True)
        stat_ref[0, 0, c : c + 1, :] = peak
        stat_ref[0, 1, c : c + 1, :] = total
    copies(stat_ref)


def plan_kernel(old_ref, colstat_ref, buf_ref, sum_ref, shift_ref, f1_ref):
    z_ref, out_ref = planes(old_ref)[0], planes(buf_ref)[0]
    nr, nc = z_ref.shape[0] // L, z_ref.shape[1] // L
    s_ref = vec(buf_ref, S)
    f1_ref[...] = vec(old_ref, F1)[...]
    lse = merged(colstat_ref)
    shift_ref[...] = -lse
    s_ref[...] = jnp.exp(lse)

    def body(r):
        shift = spread(f1_ref, r)
        waiting, totals = None, []
        for strip in range(0, L, 8):
            rs = pl.ds(pl.multiple_of(r * L + strip, 8), 8)
            row = shift[strip : strip + 8]
            values = [
                jnp.exp((z_ref[rs, cols_of(c)] + row) + shift_ref[c : c + 1, :]) for c in range(nc)
            ]
            totals.append(functools.reduce(jnp.add, values))
            put(out_ref, waiting)
            waiting = (rs, values)
        put(out_ref, waiting)
        sum_ref[0, pl.ds(r, 1), :] = fold_rows(jnp.concatenate(totals))

    each_row(nr, body, PLAN_UNROLL)
    copies(sum_ref)


def put(out_ref, waiting):
    if waiting is not None:
        for c, value in enumerate(waiting[1]):
            out_ref[waiting[0], cols_of(c)] = value


def edges_kernel(old_ref, rowsum_ref, buf_ref, stat_ref, one_ref, two_ref):
    b_ref, w_ref = planes(old_ref)[:2]
    nr, nc = b_ref.shape[0] // L, b_ref.shape[1] // L
    ib_ref = vec(buf_ref, IB)
    ib_ref[...] = 1.0 / summed(rowsum_ref)
    one_ref[...] = jnp.zeros_like(one_ref)
    two_ref[...] = jnp.zeros_like(two_ref)

    def body(r):
        rs = rows_of(r)
        inv = spread(ib_ref, r)
        for c in range(nc):
            cs = cols_of(c)
            value = b_ref[rs, cs] * inv
            one_ref[:, cs] += fold_sub(value, jnp.sum)
            two_ref[:, cs] += fold_sub(value * w_ref[rs, cs], jnp.sum)

    each_row(nr, body)
    for c in range(nc):
        cs = cols_of(c)
        stat_ref[0, 0, c : c + 1, :] = jnp.sum(one_ref[:, cs], axis=0, keepdims=True)
        stat_ref[0, 1, c : c + 1, :] = jnp.sum(two_ref[:, cs], axis=0, keepdims=True)
    copies(stat_ref)


def begin(pairs, sem):
    moves = [pltpu.make_async_copy(src, dst, sem.at[n]) for n, (src, dst) in enumerate(pairs)]
    for move in moves:
        move.start()
    return moves


def double(out_ref, r, value):
    high, low = split(value)
    chunk = out_ref.shape[2] // 2
    k, place = divmod(r * L, chunk)
    for start in (place, chunk + place):
        out_ref[k, :L, start : start + L] = high
        out_ref[k, L:, start : start + L] = low


def sweep(count, fill, use, slots):
    def both(filling, using):
        for one, other in itertools.zip_longest(filling, using):
            if one is not None:
                one()
            if other is not None:
                other()

    def body(j, carry):
        k = 2 * j
        both(fill(k + 1, slots[1]), use(k, slots[0]))
        both(fill(jnp.minimum(k + 2, count - 1), slots[0]), use(k + 1, slots[1]))
        return carry

    both(fill(0, slots[0]), [])
    lax.fori_loop(0, count // 2, body, 0)


def add_columns(left_ref, k, slot_ref, acc_ref, n):
    width = min(512, acc_ref.shape[1])
    ns = slice(n * width, (n + 1) * width)
    acc_ref[:, ns] += jnp.dot(left_ref[k], slot_ref[:, ns], preferred_element_type=F32)


def column_parts(acc_ref):
    return range(acc_ref.shape[1] // min(512, acc_ref.shape[1]))


def rowback_kernel(
    share, ratio, scale, old_ref, p_hbm, cot_hbm, colsum_ref, buf_ref, sum_ref,
    ct_ref, acc_ref, one_ref, two_ref, p_ref, cot_ref, sem
):
    moves = begin(((p_hbm, p_ref), (cot_hbm, cot_ref)), sem)
    b_ref, w_ref = planes(old_ref)[:2]
    pt_ref, direct_ref = planes(buf_ref)[2:]
    rows, cols = b_ref.shape
    nr, nc = rows // L, cols // L
    ib_ref, q_ref, h_ref = vec(old_ref, IB), vec(buf_ref, Q), vec(buf_ref, H)
    q = share / summed(colsum_ref, 0)
    q_ref[...] = q
    h_ref[...] = ratio * (q * summed(colsum_ref, 1))
    acc_ref[...] = jnp.zeros_like(acc_ref)

    def body(r):
        rs = rows_of(r)
        total = jnp.zeros((L, L), F32)
        for c in range(nc):
            cs = cols_of(c)
            total = total + (b_ref[rs, cs] * q_ref[c : c + 1, :]) * (w_ref[rs, cs] - h_ref[c : c + 1, :])
        sum_ref[0, pl.ds(r, 1), :] = fold_rows(total)

    each_row(nr, body)
    for move in moves:
        move.wait()
    for r in range(nr):
        rs = slice(r * L, (r + 1) * L)
        pt_ref[:, rs] = (p_ref[rs, :] * scale).T
        double(ct_ref, r, cot_ref[rs, :].T * ib_ref[r : r + 1, :])
    chunk = one_ref.shape[0] // 2

    def fill(k, slot_ref):
        def piece(sub):
            rs = rows_of(k * (chunk // L) + sub)
            for c in range(nc):
                high, low = split(b_ref[rs, cols_of(c)])
                slot_ref[sub * L : (sub + 1) * L, cols_of(c)] = high
                slot_ref[chunk + sub * L : chunk + (sub + 1) * L, cols_of(c)] = low

        return [functools.partial(piece, sub) for sub in range(chunk // L)]

    def use(k, slot_ref):
        return [functools.partial(add_columns, ct_ref, k, slot_ref, acc_ref, n) for n in column_parts(acc_ref)]

    sweep(rows // chunk, fill, use, (one_ref, two_ref))
    direct_ref[...] = acc_ref[:L, :] + acc_ref[L:, :]
    copies(sum_ref)


def colback_kernel(old_ref, rowsum_ref, buf_ref, sum_ref, acc_ref):
    b_ref = planes(old_ref)[0]
    nr, nc = b_ref.shape[0] // L, b_ref.shape[1] // L
    ib_ref, y_ref = vec(old_ref, IB), vec(buf_ref, Y)
    y_ref[...] = (summed(rowsum_ref) * ib_ref[...]) * ib_ref[...]
    acc_ref[...] = jnp.zeros_like(acc_ref)

    def body(r):
        rs = rows_of(r)
        y = spread(y_ref, r)
        for c in range(nc):
            cs = cols_of(c)
            acc_ref[:, cs] += fold_sub(b_ref[rs, cs] * y, jnp.sum)

    each_row(nr, body)
    for c in range(nc):
        sum_ref[0, c : c + 1, :] = -jnp.sum(acc_ref[:, cols_of(c)], axis=0, keepdims=True)
    copies(sum_ref)


def lastrow_kernel(old_ref, colsum_ref, buf_ref, sum_ref):
    b_ref = planes(old_ref)[0]
    nr, nc = b_ref.shape[0] // L, b_ref.shape[1] // L
    d_ref = vec(buf_ref, D)
    d_ref[...] = summed(colsum_ref)

    def body(r):
        rs = rows_of(r)
        total = jnp.zeros((L, L), F32)
        for c in range(nc):
            total = total + b_ref[rs, cols_of(c)] * d_ref[c : c + 1, :]
        sum_ref[0, pl.ds(r, 1), :] = -fold_rows(total)

    each_row(nr, body)
    copies(sum_ref)


def final_kernel(
    scale, old_ref, c_hbm, rowsum_ref, pg_ref, cg_ref,
    ib_ref, y_ref, f_ref, pt_ref, cc_ref, acc_ref, one_ref, two_ref, c_ref, sem
):
    moves = begin(((c_hbm, c_ref),), sem)
    b_ref, w_ref, p_ref, direct_ref = planes(old_ref)
    rows, cols = b_ref.shape
    nr, nc = rows // L, cols // L
    s_ref, q_ref, h_ref, d_ref = (vec(old_ref, name) for name in (S, Q, H, D))
    f_ref[...] = summed(rowsum_ref)
    ib_ref[...] = vec(old_ref, IB)[...]
    y_ref[...] = vec(old_ref, Y)[...]
    acc_ref[...] = jnp.zeros_like(acc_ref)
    for r in range(nr):
        double(pt_ref, r, p_ref[:, r * L : (r + 1) * L])
    for move in moves:
        move.wait()
    high, low = split(c_ref[...] * scale)
    cc_ref[:, :L] = high
    cc_ref[:, L:] = low
    chunk = one_ref.shape[0] // 2

    def fill(k, slot_ref):
        def piece(sub):
            r = k * (chunk // L) + sub
            rs = rows_of(r)
            inv, y, f = spread(ib_ref, r), spread(y_ref, r), spread(f_ref, r)
            for c in range(nc):
                row, cs = slice(c, c + 1), cols_of(c)
                plan = (q_ref[row, :] * inv) * (w_ref[rs, cs] - h_ref[row, :])
                factor = (y + d_ref[row, :]) + s_ref[row, :] * f
                high, low = split(b_ref[rs, cs] * (plan - factor))
                slot_ref[sub * L : (sub + 1) * L, cs] = high
                slot_ref[chunk + sub * L : chunk + (sub + 1) * L, cs] = low

        return [functools.partial(piece, sub) for sub in range(chunk // L)]

    def use(k, slot_ref):
        def points_part():
            both = jnp.dot(slot_ref[...], cc_ref[...], preferred_element_type=F32)
            both = both[:, :L] + both[:, L:]
            pg_ref[pl.ds(pl.multiple_of(k * chunk, chunk), chunk), :] = both[:chunk] + both[chunk:]

        parts = [functools.partial(add_columns, pt_ref, k, slot_ref, acc_ref, n) for n in column_parts(acc_ref)]
        return [points_part] + parts

    sweep(rows // chunk, fill, use, (one_ref, two_ref))
    for c in range(nc):
        cs = cols_of(c)
        plan = direct_ref[:, cs] * q_ref[c : c + 1, :]
        cg_ref[cs, :] = ((acc_ref[:L, cs] + acc_ref[L:, cs]) + plan).T


MIB = 1024 * 1024
LIMIT = 15 * MIB


def call(kernel, name, buf, fetched, args, outs, scratch=(), keep=True):
    whole = pl.BlockSpec(memory_space=pltpu.VMEM)
    outside = pl.BlockSpec(memory_space=pltpu.HBM)
    shapes = [jax.ShapeDtypeStruct(o, F32) for o in outs]
    specs = [outside] * len(fetched) + [whole] * len(args)
    args = [pltpu.with_memory_space_constraint(a, pltpu.HBM) for a in fetched] + args
    scratch = [pltpu.VMEM(s, t) for s, t in scratch]
    if fetched:
        scratch += [pltpu.VMEM(a.shape, F32) for a in fetched] + [pltpu.SemaphoreType.DMA((len(fetched),))]
    aliases = {}
    if isinstance(buf, tuple):
        shapes = [pltpu.VMEM(buf, F32)] + shapes
    else:
        args = [pltpu.with_memory_space_constraint(buf, pltpu.VMEM)] + args
        specs = [whole] + specs
        if keep:
            shapes = [pltpu.VMEM(buf.shape, F32)] + shapes
            aliases = {0: 0}
    return pl.pallas_call(
        kernel,
        name=name,
        out_shape=shapes,
        in_specs=specs,
        out_specs=[whole] * len(shapes),
        scratch_shapes=scratch,
        input_output_aliases=aliases,
        compiler_params=pltpu.CompilerParams(vmem_limit_bytes=LIMIT),
    )(*args)


def over(axis, value):
    return lax.all_to_all(value, axis, 0, 0, tiled=True)


def sizes():
    return lax.axis_size("pt"), lax.axis_size("ct")


def per_device(points, centroids, cotangent):
    rows, width = points.shape
    cols = centroids.shape[0]
    npt, nct = sizes()
    share = (rows * npt) / (cols * nct)
    ratio = (cols * nct) / (rows * npt)
    scale = 3.0 / math.sqrt(width)
    rvec, cvec = (rows // L, L), (cols // L, L)
    to_pt, to_ct = (npt,) + cvec, (nct,) + rvec
    tall = [((rows, 4 * L), BF16), ((cols, 4 * L), BF16)]
    strip = ((8, cols), F32)
    chunk = min(CHUNK, rows // 2)
    slot = ((2 * chunk, cols), BF16)
    doubles = ((rows // chunk, 2 * L, 2 * chunk), BF16)
    wide = ((2 * L, cols), F32)
    part = functools.partial

    extra = -(-7 // (cols // L)) * (cols // L)
    height = 2 * cols + 2 * L + -(-extra // 8) * 8
    buf, stat = call(
        part(scores_kernel, scale), "scores", (height, cols), [points, centroids], [],
        [(nct, 2) + rvec], tall,
    )
    stat = over("ct", stat)
    buf, stat = call(
        cols_kernel, "cols", buf, [cotangent, centroids], [stat],
        [(npt, 2) + cvec], [strip, strip] + tall,
    )
    stat = over("pt", stat)
    buf, sums = call(plan_kernel, "plan", buf, [], [stat], [to_ct], [(cvec, F32), (rvec, F32)])
    sums = over("ct", sums)
    buf, stat = call(edges_kernel, "edges", buf, [], [sums], [(npt, 2) + cvec], [strip, strip])
    stat = over("pt", stat)
    buf, sums = call(
        part(rowback_kernel, share, ratio, scale), "rowback", buf, [points, cotangent], [stat],
        [to_ct], [doubles, wide, slot, slot],
    )
    sums = over("ct", sums)
    buf, sums = call(colback_kernel, "colback", buf, [], [sums], [to_pt], [strip])
    sums = over("pt", sums)
    buf, sums = call(lastrow_kernel, "lastrow", buf, [], [sums], [to_ct])
    sums = over("ct", sums)
    pg, cg = call(
        part(final_kernel, scale), "final", buf, [centroids], [sums],
        [(rows, width), (cols, width)],
        [(rvec, F32), (rvec, F32), (rvec, F32), doubles, ((cols, 2 * L), BF16), wide, slot, slot],
        keep=False,
    )
    point_grad = gather_points(pg)
    cg = over("pt", cg.reshape(npt, cols // npt, width))
    cg = jnp.sum(cg, axis=0)
    cg = over("pt", jnp.broadcast_to(cg[None], (npt, cols // npt, width)))
    return (point_grad, cg.reshape(cols, width))


def gather_points(value):
    n = lax.axis_size("ct")
    me = lax.axis_index("ct")
    size = value.shape[0] // n
    total = lax.dynamic_slice_in_dim(value, me * size, size)
    for step in range(1, n):
        block = lax.dynamic_slice_in_dim(value, (me + step) % n * size, size)
        total = total + lax.ppermute(block, "ct", [(k, (k + step) % n) for k in range(n)])
    return total


def solution(mesh):
    return jax.shard_map(
        per_device,
        mesh=mesh,
        in_specs=(P("pt", None), P("ct", None), P("pt", None)),
        out_specs=(P(("pt", "ct"), None), P("ct", None)),
        check_vma=False,
    )
```

time: 256 us -> 173 us (0.68)
  local copies, waits for them, and re-layouts: 39 us -> 2.12 us
  Pallas kernels: 81.9 us -> 53.7 us
  waiting for transfers between devices: 32.8 us -> 8.04 us
  blocking collectives: 88.9 us -> 93.5 us
    unnamed x21 -> x1, local copies, waits for them, and re-layouts: 37.9 us -> 0.97 us
    all_to_all x3 -> x1, waiting for transfers between devices: 32.8 us -> 0.01 us  [over(): return lax.all_to_all(value, axis, 0, 0, tiled=True)]
    pallas_call x9 -> x8, Pallas kernels: 81.9 us -> 53.7 us  [call(): pl.pallas_call(kernel, name=name, out_shape=shapes, in_specs=specs, out_s...]
    ppermute x0 -> x7, waiting for transfers between devices: none -> 8.04 us  [gather_points(): lax.ppermute(block, 'ct', [(k, (k + step) % n) for k in range(n)])]
    ppermute x0 -> x7, starting transfers between devices: none -> 7.34 us  [gather_points(): lax.ppermute(block, 'ct', [(k, (k + step) % n) for k in range(n)])]
    all_to_all x3 -> x1, starting transfers between devices: 10.6 us -> 3.66 us  [over(): return lax.all_to_all(value, axis, 0, 0, tiled=True)]
    all_to_all x7 -> x8, blocking collectives: 88.9 us -> 93.5 us  [over(): return lax.all_to_all(value, axis, 0, 0, tiled=True)]
  transfers between devices with their start and end apart: 3 -> 8, of which waited for: 2 -> 6; matrix products, arithmetic and copies ran while one was open for 0% -> 1% of each run, Pallas kernels for 4% -> 0%
where the time goes in v2:
time: 173 us; the launch traced here: 171 us
  blocking collectives  93.5 us (54%)
  Pallas kernels  53.7 us (31%)
  starting transfers between devices  11 us (6%)
  waiting for transfers between devices  8.04 us (5%)
  local copies, waits for them, and re-layouts  2.12 us (1%)
    all_to_all x8, blocking collectives, over(): return lax.all_to_all(value, axis, 0, 0, tiled=True)  93.5 us
    pallas_call x8, Pallas kernels, call(): pl.pallas_call(kernel, name=name, out_shape=shapes, in_specs=specs, out_s...  53.7 us
    ppermute x7, waiting for transfers between devices, gather_points(): lax.ppermute(block, 'ct', [(k, (k + step) % n) for k in range(n)])  8.04 us
    ppermute x7, starting transfers between devices, gather_points(): lax.ppermute(block, 'ct', [(k, (k + step) % n) for k in range(n)])  7.34 us
    all_to_all x1, starting transfers between devices, over(): return lax.all_to_all(value, axis, 0, 0, tiled=True)  3.66 us
  transfers between devices with their start and end apart: 8, of which 6 were waited for; matrix products, arithmetic and copies ran while one was open for 1% of the time, Pallas kernels for 0%

profile of v2, /device:TPU:0, one launch (start us, length us, event | category | flops | bytes accessed | tf_op | source)
XLA Modules:
  0.0 170.8 jit_solution(7489696667681717459)
XLA Ops:
  0.6 8.2 %scores.1 = (f32[4368,2048]{1,0:T(8,128)S(1)}, f32[8,2,16,128]{3,2,1,0:T(8,128)S(1)}) custom-call(f32[2048,128]{1,0:T(8,128)} %p_hbm.3, f32[2048,128]{1,0:T(8,128)} %c_hbm.5), custom_call_target="tpu_custom_call" | custom-call | tf_op jit(solution)/shard_map/scores/pallas_call | solution.py:454
  8.8 11.3 %all_to_all.45.rowstat_ref = f32[8,2,16,128]{3,2,1,0:T(8,128)S(1)} all-to-all(f32[8,2,16,128]{3,2,1,0:T(8,128)S(1)} %get-tuple-element.19), channel_id=1, replica_groups=mesh['pt'=16,'ct'=8] {'ct'}, dimensions={0} | all-to-all | bytes 262144 | tf_op jit(solution)/shard_map/all_to_all | solution.py:467
  20.2 10.0 %cols.1 = (f32[4368,2048]{1,0:T(8,128)S(1)}, f32[16,2,16,128]{3,2,1,0:T(8,128)S(1)}) custom-call(f32[4368,2048]{1,0:T(8,128)S(1)} %get-tuple-element.18.old_ref, f32[2048,128]{1,0:T(8,128)} %cot_hbm.3, f32[2048,128]{1,0:T(8,128)} %c_hbm.5, f32[8,2,16,128]{3,2,1,0:T(8,128)S(1)} %all_to_all.45.rowstat_ref), custom_call_target="tpu_custom_call", output_to_operand_aliasing={{0}: (0, {})} | custom-call | tf_op jit(solution)/shard_map/cols/pallas_call | solution.py:454
  30.2 15.5 %all_to_all.46.colstat_ref = f32[16,2,16,128]{3,2,1,0:T(8,128)S(1)} all-to-all(f32[16,2,16,128]{3,2,1,0:T(8,128)S(1)} %get-tuple-element.21), channel_id=1, replica_groups=mesh['pt'=16,'ct'=8] {'pt'}, dimensions={0} | all-to-all | bytes 524288 | tf_op jit(solution)/shard_map/all_to_all | solution.py:467
  45.7 4.2 %plan.1 = (f32[4368,2048]{1,0:T(8,128)S(1)}, f32[8,16,128]{2,1,0:T(8,128)S(1)}) custom-call(f32[4368,2048]{1,0:T(8,128)S(1)} %get-tuple-element.20.old_ref, f32[16,2,16,128]{3,2,1,0:T(8,128)S(1)} %all_to_all.46.colstat_ref), custom_call_target="tpu_custom_call", output_to_operand_aliasing={{0}: (0, {})} | custom-call | tf_op jit(solution)/shard_map/plan/pallas_call | solution.py:454
  49.9 8.0 %all_to_all.47.rowsum_ref = f32[8,16,128]{2,1,0:T(8,128)S(1)} all-to-all(f32[8,16,128]{2,1,0:T(8,128)S(1)} %get-tuple-element.23), channel_id=1, replica_groups=mesh['pt'=16,'ct'=8] {'ct'}, dimensions={0} | all-to-all | bytes 131072 | tf_op jit(solution)/shard_map/all_to_all | solution.py:467
  57.9 2.5 %edges.1 = (f32[4368,2048]{1,0:T(8,128)S(1)}, f32[16,2,16,128]{3,2,1,0:T(8,128)S(1)}) custom-call(f32[4368,2048]{1,0:T(8,128)S(1)} %get-tuple-element.22.old_ref, f32[8,16,128]{2,1,0:T(8,128)S(1)} %all_to_all.47.rowsum_ref), custom_call_target="tpu_custom_call", output_to_operand_aliasing={{0}: (0, {})} | custom-call | tf_op jit(solution)/shard_map/edges/pallas_call | solution.py:454
  60.4 11.6 %all_to_all.48.colsum_ref = f32[16,2,16,128]{3,2,1,0:T(8,128)S(1)} all-to-all(f32[16,2,16,128]{3,2,1,0:T(8,128)S(1)} %get-tuple-element.25), channel_id=1, replica_groups=mesh['pt'=16,'ct'=8] {'pt'}, dimensions={0} | all-to-all | bytes 524288 | tf_op jit(solution)/shard_map/all_to_all | solution.py:467
  72.0 9.2 %rowback.1 = (f32[4368,2048]{1,0:T(8,128)S(1)}, f32[8,16,128]{2,1,0:T(8,128)S(1)}) custom-call(f32[4368,2048]{1,0:T(8,128)S(1)} %get-tuple-element.24.old_ref, f32[2048,128]{1,0:T(8,128)} %p_hbm.3, f32[2048,128]{1,0:T(8,128)} %cot_hbm.3, f32[16,2,16,128]{3,2,1,0:T(8,128)S(1)} %all_to_all.48.colsum_ref), custom_call_target="tpu_custom_call", output_to_operand_aliasing={{0}: (0, {})} | custom-call | tf_op jit(solution)/shard_map/rowback/pallas_call | solution.py:454
  81.2 8.0 %all_to_all.49.rowsum_ref = f32[8,16,128]{2,1,0:T(8,128)S(1)} all-to-all(f32[8,16,128]{2,1,0:T(8,128)S(1)} %get-tuple-element.27), channel_id=1, replica_groups=mesh['pt'=16,'ct'=8] {'ct'}, dimensions={0} | all-to-all | bytes 131072 | tf_op jit(solution)/shard_map/all_to_all | solution.py:467
  89.2 1.2 colback.1
  90.4 10.9 %all_to_all.50.colsum_ref = f32[16,16,128]{2,1,0:T(8,128)S(1)} all-to-all(f32[16,16,128]{2,1,0:T(8,128)S(1)} %get-tuple-element.29), channel_id=1, replica_groups=mesh['pt'=16,'ct'=8] {'pt'}, dimensions={0} | all-to-all | bytes 262144 | tf_op jit(solution)/shard_map/all_to_all | solution.py:467
  101.3 1.2 lastrow.1
  102.5 8.0 %all_to_all.51.rowsum_ref = f32[8,16,128]{2,1,0:T(8,128)S(1)} all-to-all(f32[8,16,128]{2,1,0:T(8,128)S(1)} %get-tuple-element.31), channel_id=1, replica_groups=mesh['pt'=16,'ct'=8] {'ct'}, dimensions={0} | all-to-all | bytes 131072 | tf_op jit(solution)/shard_map/all_to_all | solution.py:467
  110.5 17.2 %final.1 = (f32[2048,128]{1,0:T(8,128)S(1)}, f32[2048,128]{1,0:T(8,128)S(1)}) custom-call(f32[4368,2048]{1,0:T(8,128)S(1)} %get-tuple-element.30.old_ref, f32[2048,128]{1,0:T(8,128)} %c_hbm.5, f32[8,16,128]{2,1,0:T(8,128)S(1)} %all_to_all.51.rowsum_ref), custom_call_target="tpu_custom_call" | custom-call | tf_op jit(solution)/shard_map/final/pallas_call | solution.py:454
  127.7 20.1 %all_to_all.52 = f32[16,128,128]{2,1,0:T(8,128)S(1)} all-to-all(f32[16,128,128]{2,1,0:T(8,128)S(1)} %bitcast.2), channel_id=1, replica_groups=mesh['pt'=16,'ct'=8] {'pt'}, dimensions={0} | all-to-all | bytes 2097152 | tf_op jit(solution)/shard_map/all_to_all | solution.py:467
  147.9 1.1 broadcast_in_dim.2
  148.9 3.7 %all-to-all-start.8 = ((f32[16,128,128]{2,1,0:T(8,128)}), f32[16,128,128]{2,1,0:T(8,128)S(1)}, u32[]{:S(2)}, u32[]{:S(2)}) async-start(f32[16,128,128]{2,1,0:T(8,128)} %broadcast_in_dim.2), calls=%async_computation.8 | async-start | bytes 2097152 | tf_op jit(solution)/shard_map/all_to_all | solution.py:467
  152.8 0.6 collective-permute-start.1
  153.4 1.4 collective-permute-start.2
  154.8 2.7 %collective-permute-start.3 = (f32[256,128]{1,0:T(8,128)S(1)}, f32[256,128]{1,0:T(8,128)S(1)}, u32[]{:S(2)}, u32[]{:S(2)}) collective-permute-start(f32[256,128]{1,0:T(8,128)S(1)} %get-tuple-element.38), channel_id=1, source_target_pairs={{0,4},{1,5},{2,6},{3,7},{4,0},{5,1},{6,2},{7,3},{8,12},{9,13},{10,... | collective-permute-start | bytes 393224 | tf_op jit(solution)/shard_map/ppermute | solution.py:536
  157.5 1.0 collective-permute-start.4
  158.5 0.7 collective-permute-done
  159.2 0.4 collective-permute-start.5
  159.6 0.8 collective-permute-done.1
  160.4 1.3 collective-permute-start.6
  161.7 2.6 %collective-permute-done.2 = f32[256,128]{1,0:T(8,128)S(1)} collective-permute-done((f32[256,128]{1,0:T(8,128)S(1)}, f32[256,128]{1,0:T(8,128)S(1)}, u32[]{:S(2)}, u32[]{:S(2)}) %collective-permute-start.2) | collective-permute-done | bytes 131104 | tf_op jit(solution)/shard_map/ppermute | solution.py:536
  164.3 1.2 collective-permute-done.3
  165.5 1.7 %collective-permute-done.5 = f32[256,128]{1,0:T(8,128)S(1)} collective-permute-done((f32[256,128]{1,0:T(8,128)S(1)}, f32[256,128]{1,0:T(8,128)S(1)}, u32[]{:S(2)}, u32[]{:S(2)}) %collective-permute-start.5) | collective-permute-done | bytes 131104 | tf_op jit(solution)/shard_map/ppermute | solution.py:536
  167.3 0.9 collective-permute-done.6
  168.2 1.6 add_add_fusion
  169.8 1.0 copy.18
  (5 shorter events, 0.2 us)
Async XLA Ops:
  148.9 20.9 %all-to-all-start.8 = ((f32[16,128,128]{2,1,0:T(8,128)}), f32[16,128,128]{2,1,0:T(8,128)S(1)}, u32[]{:S(2)}, u32[]{:S(2)}) async-start(f32[16,128,128]{2,1,0:T(8,128)} %broadcast_in_dim.2), calls=%async_computation.8 | async-start | bytes 2097152 | tf_op jit(solution)/shard_map/all_to_all | solution.py:467
  152.8 6.4 %collective-permute-start = (f32[256,128]{1,0:T(8,128)S(1)}, f32[256,128]{1,0:T(8,128)S(1)}, u32[]{:S(2)}, u32[]{:S(2)}) collective-permute-start(f32[256,128]{1,0:T(8,128)S(1)} %get-tuple-element.34), channel_id=1, source_target_pairs={{0,1},{1,2},{2,3},{3,4},{4,5},{5,6},{6,7},{7,0},{8,9},{9,10},{10,1... | collective-permute-start | bytes 393224 | tf_op jit(solution)/shard_map/ppermute | solution.py:536
  152.8 7.6 %collective-permute-start.1 = (f32[256,128]{1,0:T(8,128)S(1)}, f32[256,128]{1,0:T(8,128)S(1)}, u32[]{:S(2)}, u32[]{:S(2)}) collective-permute-start(f32[256,128]{1,0:T(8,128)S(1)} %get-tuple-element.40), channel_id=1, source_target_pairs={{0,2},{1,3},{2,4},{3,5},{4,6},{5,7},{6,0},{7,1},{8,10},{9,11},{10,... | collective-permute-start | bytes 393224 | tf_op jit(solution)/shard_map/ppermute | solution.py:536
  153.4 10.8 %collective-permute-start.2 = (f32[256,128]{1,0:T(8,128)S(1)}, f32[256,128]{1,0:T(8,128)S(1)}, u32[]{:S(2)}, u32[]{:S(2)}) collective-permute-start(f32[256,128]{1,0:T(8,128)S(1)} %get-tuple-element.39), channel_id=1, source_target_pairs={{0,3},{1,4},{2,5},{3,6},{4,7},{5,0},{6,1},{7,2},{8,11},{9,12},{10,... | collective-permute-start | bytes 393224 | tf_op jit(solution)/shard_map/ppermute | solution.py:536
  154.8 10.7 %collective-permute-start.3 = (f32[256,128]{1,0:T(8,128)S(1)}, f32[256,128]{1,0:T(8,128)S(1)}, u32[]{:S(2)}, u32[]{:S(2)}) collective-permute-start(f32[256,128]{1,0:T(8,128)S(1)} %get-tuple-element.38), channel_id=1, source_target_pairs={{0,4},{1,5},{2,6},{3,7},{4,0},{5,1},{6,2},{7,3},{8,12},{9,13},{10,... | collective-permute-start | bytes 393224 | tf_op jit(solution)/shard_map/ppermute | solution.py:536
  157.5 8.0 %collective-permute-start.4 = (f32[256,128]{1,0:T(8,128)S(1)}, f32[256,128]{1,0:T(8,128)S(1)}, u32[]{:S(2)}, u32[]{:S(2)}) collective-permute-start(f32[256,128]{1,0:T(8,128)S(1)} %get-tuple-element.37), channel_id=1, source_target_pairs={{0,5},{1,6},{2,7},{3,0},{4,1},{5,2},{6,3},{7,4},{8,13},{9,14},{10,... | collective-permute-start | bytes 393224 | tf_op jit(solution)/shard_map/ppermute | solution.py:536
  159.2 8.1 %collective-permute-start.5 = (f32[256,128]{1,0:T(8,128)S(1)}, f32[256,128]{1,0:T(8,128)S(1)}, u32[]{:S(2)}, u32[]{:S(2)}) collective-permute-start(f32[256,128]{1,0:T(8,128)S(1)} %get-tuple-element.36), channel_id=1, source_target_pairs={{0,6},{1,7},{2,0},{3,1},{4,2},{5,3},{6,4},{7,5},{8,14},{9,15},{10,... | collective-permute-start | bytes 393224 | tf_op jit(solution)/shard_map/ppermute | solution.py:536
  160.4 7.8 %collective-permute-start.6 = (f32[256,128]{1,0:T(8,128)S(1)}, f32[256,128]{1,0:T(8,128)}, u32[]{:S(2)}, u32[]{:S(2)}) collective-permute-start(f32[256,128]{1,0:T(8,128)S(1)} %get-tuple-element.35), channel_id=1, source_target_pairs={{0,7},{1,0},{2,1},{3,2},{4,3},{5,4},{6,5},{7,6},{8,15},{9,8},{10,9... | collective-permute-start | bytes 393224 | tf_op jit(solution)/shard_map/ppermute | solution.py:536

commit v3 on v2

--- a/solution.py
+++ b/solution.py
@@ -15,6 +15,9 @@
 ROW_UNROLL = 16
 PLAN_UNROLL = 2
 CHUNK = 256
+GROUP = 2
+PART = (512, 512)
+WIDE = 512
 
 
 def split(x):
@@ -54,21 +57,25 @@
         out_ref[n] = out_ref[0]
 
 
-def pack(left_ref, right_ref, a_ref, b_ref, scale):
-    high, low = split(left_ref[...] * scale)
-    for k, part in enumerate((high, high, low, low)):
-        a_ref[:, cols_of(k)] = part
-    high, low = split(right_ref[...])
-    for k, part in enumerate((high, low, high, low)):
-        b_ref[:, cols_of(k)] = part
-
-
-def tiles(a_ref, b_ref, out_ref, rs, tile):
-    cols = b_ref.shape[0]
-    for c in range(0, cols, tile):
-        out_ref[rs, c : c + tile] = lax.dot_general(
-            a_ref[rs, :], b_ref[c : c + tile, :], (((1,), (1,)), ((), ())), preferred_element_type=F32
-        )
+LEFT, RIGHT = (0, 0, 1, 1), (0, 1, 0, 1)
+
+
+def pack(value_ref, out_ref, order, scale):
+    terms = split(value_ref[...] * scale)
+    for k, term in enumerate(order):
+        out_ref[:, cols_of(k)] = terms[term]
+
+
+def parts_of(rows, cols):
+    for r in range(0, rows, min(PART[0], rows)):
+        for c in range(0, cols, min(PART[1], cols)):
+            yield slice(r, r + min(PART[0], rows)), slice(c, c + min(PART[1], cols))
+
+
+def tile(a_ref, b_ref, out_ref, rs, cs):
+    out_ref[rs, cs] = lax.dot_general(
+        a_ref[rs, :], b_ref[cs, :], (((1,), (1,)), ((), ())), preferred_element_type=F32
+    )
 
 
 def each_row(nr, body, unroll=ROW_UNROLL):
@@ -84,12 +91,11 @@
     lax.fori_loop(0, nr, step, 0, unroll=min(unroll, nr))
 
 
-def fetch(pairs, sem):
+def begin(pairs, sem):
     moves = [pltpu.make_async_copy(src, dst, sem.at[n]) for n, (src, dst) in enumerate(pairs)]
     for move in moves:
         move.start()
-    for move in moves:
-        move.wait()
+    return moves
 
 
 def planes(buf_ref):
@@ -110,35 +116,52 @@
 
 
 def scores_kernel(scale, p_hbm, c_hbm, buf_ref, stat_ref, a_ref, b_ref, p_ref, c_ref, sem):
-    fetch(((p_hbm, p_ref), (c_hbm, c_ref)), sem)
-    pack(p_ref, c_ref, a_ref, b_ref, scale)
+    moves = begin(((p_hbm, p_ref), (c_hbm, c_ref)), sem)
+    moves[0].wait()
+    pack(p_ref, a_ref, LEFT, scale)
+    moves[1].wait()
+    pack(c_ref, b_ref, RIGHT, 1.0)
     z_ref = planes(buf_ref)[0]
-    rows, nc = z_ref.shape[0], z_ref.shape[1] // L
-    chunk = min(512, rows)
-    for start in range(0, rows, chunk):
-        tiles(a_ref, b_ref, z_ref, slice(start, start + chunk), min(1024, nc * L))
-        for r in range(start // L, (start + chunk) // L):
-            rs = slice(r * L, (r + 1) * L)
-            top = z_ref[rs, cols_of(0)]
-            for c in range(1, nc):
-                top = jnp.maximum(top, z_ref[rs, cols_of(c)])
-            peak = jnp.max(top.T, axis=0, keepdims=True)
-            wide = jnp.broadcast_to(peak, (L, L)).T
-            total = jnp.zeros((L, L), F32)
-            for c in range(nc):
-                total = total + jnp.exp(z_ref[rs, cols_of(c)] - wide)
-            stat_ref[0, 0, r : r + 1, :] = peak
-            stat_ref[0, 1, r : r + 1, :] = fold_rows(total)
+    rows, cols = z_ref.shape
+    nc = cols // L
+    chunk = min(PART[0], rows)
+
+    def sweep_row(r):
+        rs = slice(r * L, (r + 1) * L)
+        top = z_ref[rs, cols_of(0)]
+        for c in range(1, nc):
+            top = jnp.maximum(top, z_ref[rs, cols_of(c)])
+        peak = jnp.max(top.T, axis=0, keepdims=True)
+        wide = jnp.broadcast_to(peak, (L, L)).T
+        total = jnp.zeros((L, L), F32)
+        for c in range(nc):
+            total = total + jnp.exp(z_ref[rs, cols_of(c)] - wide)
+        stat_ref[0, r : r + 1, :] = peak + jnp.log(fold_rows(total))
+
+    products = list(parts_of(rows, cols))
+    each = len(products) * chunk // rows
+    for rs, cs in products[:each]:
+        tile(a_ref, b_ref, z_ref, rs, cs)
+    for n in range(rows // chunk):
+        coming = products[(n + 1) * each : (n + 2) * each]
+        here = range(n * chunk // L, (n + 1) * chunk // L)
+        done = 0
+        for m, r in enumerate(here):
+            until = len(coming) * (m + 1) // len(here)
+            for rs, cs in coming[done:until]:
+                tile(a_ref, b_ref, z_ref, rs, cs)
+            done = until
+            sweep_row(r)
     copies(stat_ref)
 
 
-def merged(stat_ref):
-    peak = stat_ref[0, 0]
-    for n in range(1, stat_ref.shape[0]):
-        peak = jnp.maximum(peak, stat_ref[n, 0])
+def merged(lse_ref):
+    peak = lse_ref[0]
+    for n in range(1, lse_ref.shape[0]):
+        peak = jnp.maximum(peak, lse_ref[n])
     total = jnp.zeros_like(peak)
-    for n in range(stat_ref.shape[0]):
-        total = total + stat_ref[n, 1] * jnp.exp(stat_ref[n, 0] - peak)
+    for n in range(lse_ref.shape[0]):
+        total = total + jnp.exp(lse_ref[n] - peak)
     return peak + jnp.log(total)
 
 
@@ -153,7 +176,7 @@
     old_ref, cot_hbm, c_hbm, rowstat_ref, buf_ref, stat_ref, peak_ref, total_ref, left_ref, right_ref,
     cot_ref, c_ref, sem
 ):
-    fetch(((cot_hbm, cot_ref), (c_hbm, c_ref)), sem)
+    moves = begin(((cot_hbm, cot_ref), (c_hbm, c_ref)), sem)
     b_ref = planes(old_ref)[0]
     w_ref = planes(buf_ref)[1]
     rows, cols = b_ref.shape
@@ -162,27 +185,40 @@
     f1_ref[...] = -merged(rowstat_ref)
     peak_ref[...] = jnp.full_like(peak_ref, -jnp.inf)
     total_ref[...] = jnp.zeros_like(total_ref)
-    pack(cot_ref, c_ref, left_ref, right_ref, 1.0)
-    chunk = min(512, rows)
-    for start in range(0, rows, chunk):
-        tiles(left_ref, right_ref, w_ref, slice(start, start + chunk), min(1024, cols))
-        for r in range(start // L, (start + chunk) // L):
-            rs = slice(r * L, (r + 1) * L)
-            shift = spread(f1_ref, r)
-            for c in range(nc):
-                cs = cols_of(c)
-                shifted = b_ref[rs, cs] + shift
-                old = peak_ref[:, cs]
-                new = jnp.maximum(old, fold_sub(shifted, jnp.max))
-                terms = jnp.exp(shifted.reshape(L // 8, 8, L) - new[None])
-                total_ref[:, cs] = total_ref[:, cs] * jnp.exp(old - new) + jnp.sum(terms, axis=0)
-                peak_ref[:, cs] = new
+
+    def sweep_row(r):
+        rs = slice(r * L, (r + 1) * L)
+        shift = spread(f1_ref, r)
+        for c in range(nc):
+            cs = cols_of(c)
+            shifted = b_ref[rs, cs] + shift
+            old = peak_ref[:, cs]
+            new = jnp.maximum(old, fold_sub(shifted, jnp.max))
+            terms = jnp.exp(shifted.reshape(L // 8, 8, L) - new[None])
+            total_ref[:, cs] = total_ref[:, cs] * jnp.exp(old - new) + jnp.sum(terms, axis=0)
+            peak_ref[:, cs] = new
+
+    nr = rows // L
+    early = nr // 4
+    for r in range(early):
+        sweep_row(r)
+    for move in moves:
+        move.wait()
+    pack(cot_ref, left_ref, LEFT, 1.0)
+    pack(c_ref, right_ref, RIGHT, 1.0)
+    products = list(parts_of(rows, cols))
+    done = 0
+    for n, r in enumerate(range(early, nr)):
+        until = len(products) * (n + 1) // (nr - early)
+        for rs, cs in products[done:until]:
+            tile(left_ref, right_ref, w_ref, rs, cs)
+        done = until
+        sweep_row(r)
     for c in range(nc):
         cs = cols_of(c)
         peak = jnp.max(peak_ref[:, cs], axis=0, keepdims=True)
         total = jnp.sum(total_ref[:, cs] * jnp.exp(peak_ref[:, cs] - peak), axis=0, keepdims=True)
-        stat_ref[0, 0, c : c + 1, :] = peak
-        stat_ref[0, 1, c : c + 1, :] = total
+        stat_ref[0, c : c + 1, :] = peak + jnp.log(total)
     copies(stat_ref)
 
 
@@ -245,13 +281,6 @@
     copies(stat_ref)
 
 
-def begin(pairs, sem):
-    moves = [pltpu.make_async_copy(src, dst, sem.at[n]) for n, (src, dst) in enumerate(pairs)]
-    for move in moves:
-        move.start()
-    return moves
-
-
 def double(out_ref, r, value):
     high, low = split(value)
     chunk = out_ref.shape[2] // 2
@@ -279,14 +308,19 @@
     lax.fori_loop(0, count // 2, body, 0)
 
 
+def pieces(piece, count, nc):
+    groups = [range(c, min(c + GROUP, nc)) for c in range(0, nc, GROUP)]
+    return [functools.partial(piece, sub, group) for sub in range(count) for group in groups]
+
+
 def add_columns(left_ref, k, slot_ref, acc_ref, n):
-    width = min(512, acc_ref.shape[1])
+    width = min(WIDE, acc_ref.shape[1])
     ns = slice(n * width, (n + 1) * width)
     acc_ref[:, ns] += jnp.dot(left_ref[k], slot_ref[:, ns], preferred_element_type=F32)
 
 
 def column_parts(acc_ref):
-    return range(acc_ref.shape[1] // min(512, acc_ref.shape[1]))
+    return range(acc_ref.shape[1] // min(WIDE, acc_ref.shape[1]))
 
 
 def rowback_kernel(
@@ -322,14 +356,14 @@
     chunk = one_ref.shape[0] // 2
 
     def fill(k, slot_ref):
-        def piece(sub):
+        def piece(sub, group):
             rs = rows_of(k * (chunk // L) + sub)
-            for c in range(nc):
+            for c in group:
                 high, low = split(b_ref[rs, cols_of(c)])
                 slot_ref[sub * L : (sub + 1) * L, cols_of(c)] = high
                 slot_ref[chunk + sub * L : chunk + (sub + 1) * L, cols_of(c)] = low
 
-        return [functools.partial(piece, sub) for sub in range(chunk // L)]
+        return pieces(piece, chunk // L, nc)
 
     def use(k, slot_ref):
         return [functools.partial(add_columns, ct_ref, k, slot_ref, acc_ref, n) for n in column_parts(acc_ref)]
@@ -399,11 +433,11 @@
     chunk = one_ref.shape[0] // 2
 
     def fill(k, slot_ref):
-        def piece(sub):
+        def piece(sub, group):
             r = k * (chunk // L) + sub
             rs = rows_of(r)
             inv, y, f = spread(ib_ref, r), spread(y_ref, r), spread(f_ref, r)
-            for c in range(nc):
+            for c in group:
                 row, cs = slice(c, c + 1), cols_of(c)
                 plan = (q_ref[row, :] * inv) * (w_ref[rs, cs] - h_ref[row, :])
                 factor = (y + d_ref[row, :]) + s_ref[row, :] * f
@@ -411,7 +445,7 @@
                 slot_ref[sub * L : (sub + 1) * L, cs] = high
                 slot_ref[chunk + sub * L : chunk + (sub + 1) * L, cs] = low
 
-        return [functools.partial(piece, sub) for sub in range(chunk // L)]
+        return pieces(piece, chunk // L, nc)
 
     def use(k, slot_ref):
         def points_part():
@@ -492,12 +526,12 @@
     height = 2 * cols + 2 * L + -(-extra // 8) * 8
     buf, stat = call(
         part(scores_kernel, scale), "scores", (height, cols), [points, centroids], [],
-        [(nct, 2) + rvec], tall,
+        [to_ct], tall,
     )
     stat = over("ct", stat)
     buf, stat = call(
         cols_kernel, "cols", buf, [cotangent, centroids], [stat],
-        [(npt, 2) + cvec], [strip, strip] + tall,
+        [to_pt], [strip, strip] + tall,
     )
     stat = over("pt", stat)
     buf, sums = call(plan_kernel, "plan", buf, [], [stat], [to_ct], [(cvec, F32), (rvec, F32)])

time: 173 us -> 169 us (0.977)
  Pallas kernels: 53.7 us -> 50.2 us
    pallas_call x8, Pallas kernels: 53.7 us -> 50.2 us  [call(): pl.pallas_call(kernel, name=name, out_shape=shapes, in_specs=specs, out_s...]
where the time goes in v3:
time: 169 us; the launch traced here: 166 us
  blocking collectives  92.4 us (55%)
  Pallas kernels  50.2 us (30%)
  starting transfers between devices  11 us (7%)
  waiting for transfers between devices  8.02 us (5%)
  local copies, waits for them, and re-layouts  2.12 us (1%)
    all_to_all x8, blocking collectives, over(): return lax.all_to_all(value, axis, 0, 0, tiled=True)  92.4 us
    pallas_call x8, Pallas kernels, call(): pl.pallas_call(kernel, name=name, out_shape=shapes, in_specs=specs, out_s...  50.2 us
    ppermute x7, waiting for transfers between devices, gather_points(): lax.ppermute(block, 'ct', [(k, (k + step) % n) for k in range(n)])  8.02 us
    ppermute x7, starting transfers between devices, gather_points(): lax.ppermute(block, 'ct', [(k, (k + step) % n) for k in range(n)])  7.35 us
    all_to_all x1, starting transfers between devices, over(): return lax.all_to_all(value, axis, 0, 0, tiled=True)  3.66 us
  transfers between devices with their start and end apart: 8, of which 6 were waited for; matrix products, arithmetic and copies ran while one was open for 1% of the time, Pallas kernels for 0%

profile of v3, /device:TPU:0, one launch (start us, length us, event | category | flops | bytes accessed | tf_op | source)
XLA Modules:
  0.0 166.2 jit_solution(12821234176205471328)
XLA Ops:
  0.6 8.1 %scores.1 = (f32[4368,2048]{1,0:T(8,128)S(1)}, f32[8,16,128]{2,1,0:T(8,128)S(1)}) custom-call(f32[2048,128]{1,0:T(8,128)} %p_hbm.3, f32[2048,128]{1,0:T(8,128)} %c_hbm.5), custom_call_target="tpu_custom_call" | custom-call | tf_op jit(solution)/shard_map/scores/pallas_call | solution.py:488
  8.7 10.8 %all_to_all.45.rowstat_ref = f32[8,16,128]{2,1,0:T(8,128)S(1)} all-to-all(f32[8,16,128]{2,1,0:T(8,128)S(1)} %get-tuple-element.19), channel_id=1, replica_groups=mesh['pt'=16,'ct'=8] {'ct'}, dimensions={0} | all-to-all | bytes 131072 | tf_op jit(solution)/shard_map/all_to_all | solution.py:501
  19.5 8.8 %cols.1 = (f32[4368,2048]{1,0:T(8,128)S(1)}, f32[16,16,128]{2,1,0:T(8,128)S(1)}) custom-call(f32[4368,2048]{1,0:T(8,128)S(1)} %get-tuple-element.18.old_ref, f32[2048,128]{1,0:T(8,128)} %cot_hbm.3, f32[2048,128]{1,0:T(8,128)} %c_hbm.5, f32[8,16,128]{2,1,0:T(8,128)S(1)} %all_to_all.45.rowstat_ref), custom_call_target="tpu_custom_call", output_to_operand_aliasing={{0}: (0, {})} | custom-call | tf_op jit(solution)/shard_map/cols/pallas_call | solution.py:488
  28.4 14.8 %all_to_all.46.colstat_ref = f32[16,16,128]{2,1,0:T(8,128)S(1)} all-to-all(f32[16,16,128]{2,1,0:T(8,128)S(1)} %get-tuple-element.21), channel_id=1, replica_groups=mesh['pt'=16,'ct'=8] {'pt'}, dimensions={0} | all-to-all | bytes 262144 | tf_op jit(solution)/shard_map/all_to_all | solution.py:501
  43.2 4.2 %plan.1 = (f32[4368,2048]{1,0:T(8,128)S(1)}, f32[8,16,128]{2,1,0:T(8,128)S(1)}) custom-call(f32[4368,2048]{1,0:T(8,128)S(1)} %get-tuple-element.20.old_ref, f32[16,16,128]{2,1,0:T(8,128)S(1)} %all_to_all.46.colstat_ref), custom_call_target="tpu_custom_call", output_to_operand_aliasing={{0}: (0, {})} | custom-call | tf_op jit(solution)/shard_map/plan/pallas_call | solution.py:488
  47.4 8.0 %all_to_all.47.rowsum_ref = f32[8,16,128]{2,1,0:T(8,128)S(1)} all-to-all(f32[8,16,128]{2,1,0:T(8,128)S(1)} %get-tuple-element.23), channel_id=1, replica_groups=mesh['pt'=16,'ct'=8] {'ct'}, dimensions={0} | all-to-all | bytes 131072 | tf_op jit(solution)/shard_map/all_to_all | solution.py:501
  55.4 2.5 %edges.1 = (f32[4368,2048]{1,0:T(8,128)S(1)}, f32[16,2,16,128]{3,2,1,0:T(8,128)S(1)}) custom-call(f32[4368,2048]{1,0:T(8,128)S(1)} %get-tuple-element.22.old_ref, f32[8,16,128]{2,1,0:T(8,128)S(1)} %all_to_all.47.rowsum_ref), custom_call_target="tpu_custom_call", output_to_operand_aliasing={{0}: (0, {})} | custom-call | tf_op jit(solution)/shard_map/edges/pallas_call | solution.py:488
  57.9 11.8 %all_to_all.48.colsum_ref = f32[16,2,16,128]{3,2,1,0:T(8,128)S(1)} all-to-all(f32[16,2,16,128]{3,2,1,0:T(8,128)S(1)} %get-tuple-element.25), channel_id=1, replica_groups=mesh['pt'=16,'ct'=8] {'pt'}, dimensions={0} | all-to-all | bytes 524288 | tf_op jit(solution)/shard_map/all_to_all | solution.py:501
  69.7 9.2 %rowback.1 = (f32[4368,2048]{1,0:T(8,128)S(1)}, f32[8,16,128]{2,1,0:T(8,128)S(1)}) custom-call(f32[4368,2048]{1,0:T(8,128)S(1)} %get-tuple-element.24.old_ref, f32[2048,128]{1,0:T(8,128)} %p_hbm.3, f32[2048,128]{1,0:T(8,128)} %cot_hbm.3, f32[16,2,16,128]{3,2,1,0:T(8,128)S(1)} %all_to_all.48.colsum_ref), custom_call_target="tpu_custom_call", output_to_operand_aliasing={{0}: (0, {})} | custom-call | tf_op jit(solution)/shard_map/rowback/pallas_call | solution.py:488
  78.8 8.0 %all_to_all.49.rowsum_ref = f32[8,16,128]{2,1,0:T(8,128)S(1)} all-to-all(f32[8,16,128]{2,1,0:T(8,128)S(1)} %get-tuple-element.27), channel_id=1, replica_groups=mesh['pt'=16,'ct'=8] {'ct'}, dimensions={0} | all-to-all | bytes 131072 | tf_op jit(solution)/shard_map/all_to_all | solution.py:501
  86.8 1.2 colback.1
  88.1 10.9 %all_to_all.50.colsum_ref = f32[16,16,128]{2,1,0:T(8,128)S(1)} all-to-all(f32[16,16,128]{2,1,0:T(8,128)S(1)} %get-tuple-element.29), channel_id=1, replica_groups=mesh['pt'=16,'ct'=8] {'pt'}, dimensions={0} | all-to-all | bytes 262144 | tf_op jit(solution)/shard_map/all_to_all | solution.py:501
  98.9 1.2 lastrow.1
  100.1 8.0 %all_to_all.51.rowsum_ref = f32[8,16,128]{2,1,0:T(8,128)S(1)} all-to-all(f32[8,16,128]{2,1,0:T(8,128)S(1)} %get-tuple-element.31), channel_id=1, replica_groups=mesh['pt'=16,'ct'=8] {'ct'}, dimensions={0} | all-to-all | bytes 131072 | tf_op jit(solution)/shard_map/all_to_all | solution.py:501
  108.1 15.0 %final.1 = (f32[2048,128]{1,0:T(8,128)S(1)}, f32[2048,128]{1,0:T(8,128)S(1)}) custom-call(f32[4368,2048]{1,0:T(8,128)S(1)} %get-tuple-element.30.old_ref, f32[2048,128]{1,0:T(8,128)} %c_hbm.5, f32[8,16,128]{2,1,0:T(8,128)S(1)} %all_to_all.51.rowsum_ref), custom_call_target="tpu_custom_call" | custom-call | tf_op jit(solution)/shard_map/final/pallas_call | solution.py:488
  123.1 20.1 %all_to_all.52 = f32[16,128,128]{2,1,0:T(8,128)S(1)} all-to-all(f32[16,128,128]{2,1,0:T(8,128)S(1)} %bitcast.2), channel_id=1, replica_groups=mesh['pt'=16,'ct'=8] {'pt'}, dimensions={0} | all-to-all | bytes 2097152 | tf_op jit(solution)/shard_map/all_to_all | solution.py:501
  143.3 1.1 broadcast_in_dim.2
  144.4 3.7 %all-to-all-start.8 = ((f32[16,128,128]{2,1,0:T(8,128)}), f32[16,128,128]{2,1,0:T(8,128)S(1)}, u32[]{:S(2)}, u32[]{:S(2)}) async-start(f32[16,128,128]{2,1,0:T(8,128)} %broadcast_in_dim.2), calls=%async_computation.8 | async-start | bytes 2097152 | tf_op jit(solution)/shard_map/all_to_all | solution.py:501
  148.3 0.6 collective-permute-start.1
  148.9 1.4 collective-permute-start.2
  150.3 2.7 %collective-permute-start.3 = (f32[256,128]{1,0:T(8,128)S(1)}, f32[256,128]{1,0:T(8,128)S(1)}, u32[]{:S(2)}, u32[]{:S(2)}) collective-permute-start(f32[256,128]{1,0:T(8,128)S(1)} %get-tuple-element.38), channel_id=1, source_target_pairs={{0,4},{1,5},{2,6},{3,7},{4,0},{5,1},{6,2},{7,3},{8,12},{9,13},{10,... | collective-permute-start | bytes 393224 | tf_op jit(solution)/shard_map/ppermute | solution.py:570
  153.0 1.0 collective-permute-start.4
  153.9 0.7 collective-permute-done
  154.6 0.4 collective-permute-start.5
  155.0 0.8 collective-permute-done.1
  155.9 1.3 collective-permute-start.6
  157.1 2.6 %collective-permute-done.2 = f32[256,128]{1,0:T(8,128)S(1)} collective-permute-done((f32[256,128]{1,0:T(8,128)S(1)}, f32[256,128]{1,0:T(8,128)S(1)}, u32[]{:S(2)}, u32[]{:S(2)}) %collective-permute-start.2) | collective-permute-done | bytes 131104 | tf_op jit(solution)/shard_map/ppermute | solution.py:570
  159.7 1.2 collective-permute-done.3
  161.0 1.7 %collective-permute-done.5 = f32[256,128]{1,0:T(8,128)S(1)} collective-permute-done((f32[256,128]{1,0:T(8,128)S(1)}, f32[256,128]{1,0:T(8,128)S(1)}, u32[]{:S(2)}, u32[]{:S(2)}) %collective-permute-start.5) | collective-permute-done | bytes 131104 | tf_op jit(solution)/shard_map/ppermute | solution.py:570
  162.7 0.9 collective-permute-done.6
  163.6 1.6 add_add_fusion
  165.2 1.0 copy.18
  (5 shorter events, 0.2 us)
Async XLA Ops:
  144.4 20.9 %all-to-all-start.8 = ((f32[16,128,128]{2,1,0:T(8,128)}), f32[16,128,128]{2,1,0:T(8,128)S(1)}, u32[]{:S(2)}, u32[]{:S(2)}) async-start(f32[16,128,128]{2,1,0:T(8,128)} %broadcast_in_dim.2), calls=%async_computation.8 | async-start | bytes 2097152 | tf_op jit(solution)/shard_map/all_to_all | solution.py:501
  148.2 6.4 %collective-permute-start = (f32[256,128]{1,0:T(8,128)S(1)}, f32[256,128]{1,0:T(8,128)S(1)}, u32[]{:S(2)}, u32[]{:S(2)}) collective-permute-start(f32[256,128]{1,0:T(8,128)S(1)} %get-tuple-element.34), channel_id=1, source_target_pairs={{0,1},{1,2},{2,3},{3,4},{4,5},{5,6},{6,7},{7,0},{8,9},{9,10},{10,1... | collective-permute-start | bytes 393224 | tf_op jit(solution)/shard_map/ppermute | solution.py:570
  148.3 7.6 %collective-permute-start.1 = (f32[256,128]{1,0:T(8,128)S(1)}, f32[256,128]{1,0:T(8,128)S(1)}, u32[]{:S(2)}, u32[]{:S(2)}) collective-permute-start(f32[256,128]{1,0:T(8,128)S(1)} %get-tuple-element.40), channel_id=1, source_target_pairs={{0,2},{1,3},{2,4},{3,5},{4,6},{5,7},{6,0},{7,1},{8,10},{9,11},{10,... | collective-permute-start | bytes 393224 | tf_op jit(solution)/shard_map/ppermute | solution.py:570
  148.9 10.8 %collective-permute-start.2 = (f32[256,128]{1,0:T(8,128)S(1)}, f32[256,128]{1,0:T(8,128)S(1)}, u32[]{:S(2)}, u32[]{:S(2)}) collective-permute-start(f32[256,128]{1,0:T(8,128)S(1)} %get-tuple-element.39), channel_id=1, source_target_pairs={{0,3},{1,4},{2,5},{3,6},{4,7},{5,0},{6,1},{7,2},{8,11},{9,12},{10,... | collective-permute-start | bytes 393224 | tf_op jit(solution)/shard_map/ppermute | solution.py:570
  150.3 10.7 %collective-permute-start.3 = (f32[256,128]{1,0:T(8,128)S(1)}, f32[256,128]{1,0:T(8,128)S(1)}, u32[]{:S(2)}, u32[]{:S(2)}) collective-permute-start(f32[256,128]{1,0:T(8,128)S(1)} %get-tuple-element.38), channel_id=1, source_target_pairs={{0,4},{1,5},{2,6},{3,7},{4,0},{5,1},{6,2},{7,3},{8,12},{9,13},{10,... | collective-permute-start | bytes 393224 | tf_op jit(solution)/shard_map/ppermute | solution.py:570
  153.0 8.0 %collective-permute-start.4 = (f32[256,128]{1,0:T(8,128)S(1)}, f32[256,128]{1,0:T(8,128)S(1)}, u32[]{:S(2)}, u32[]{:S(2)}) collective-permute-start(f32[256,128]{1,0:T(8,128)S(1)} %get-tuple-element.37), channel_id=1, source_target_pairs={{0,5},{1,6},{2,7},{3,0},{4,1},{5,2},{6,3},{7,4},{8,13},{9,14},{10,... | collective-permute-start | bytes 393224 | tf_op jit(solution)/shard_map/ppermute | solution.py:570
  154.6 8.1 %collective-permute-start.5 = (f32[256,128]{1,0:T(8,128)S(1)}, f32[256,128]{1,0:T(8,128)S(1)}, u32[]{:S(2)}, u32[]{:S(2)}) collective-permute-start(f32[256,128]{1,0:T(8,128)S(1)} %get-tuple-element.36), channel_id=1, source_target_pairs={{0,6},{1,7},{2,0},{3,1},{4,2},{5,3},{6,4},{7,5},{8,14},{9,15},{10,... | collective-permute-start | bytes 393224 | tf_op jit(solution)/shard_map/ppermute | solution.py:570
  155.9 7.8 %collective-permute-start.6 = (f32[256,128]{1,0:T(8,128)S(1)}, f32[256,128]{1,0:T(8,128)}, u32[]{:S(2)}, u32[]{:S(2)}) collective-permute-start(f32[256,128]{1,0:T(8,128)S(1)} %get-tuple-element.35), channel_id=1, source_target_pairs={{0,7},{1,0},{2,1},{3,2},{4,3},{5,4},{6,5},{7,6},{8,15},{9,8},{10,9... | collective-permute-start | bytes 393224 | tf_op jit(solution)/shard_map/ppermute | solution.py:570
